TPU v7x, 32 devices: a whole 2x2x4 slice. The times are simulated.
32 devices in a mesh: dp: 8 (over z, y), seq: 4 (over x, core).
Axes of the slice: x: 2, y: 2, z: 4, core: 2. Of those that a mesh axis runs over, the one named last changes fastest.
Arguments:
- tokens: bfloat16 [8, 2048, 1024], P('dp', 'seq'), may hold values from -6 to 6
- cotangent: bfloat16 [8, 2048, 1024], P('dp', 'seq'), may hold values from -6 to 6
- in_weight: bfloat16 [1024, 4384], P('dp'), may hold values from -0.1875 to 0.1875
- out_weight: bfloat16 [2048, 1024], P('dp'), may hold values from -0.125 to 0.125
- conv_weight: bfloat16 [4, 2304], P(None, 'dp'), may hold values from -3 to 3
- conv_bias: bfloat16 [2304], P('dp'), may hold values from -0.5 to 0.5
- pre_gain: bfloat16 [1024], P('dp'), may hold values from 0.5 to 1.5
- norm_gain: bfloat16 [2048], P('dp'), may hold values from 0.5 to 1.5
- step_bias: bfloat16 [32], P('dp'), may hold values from -4 to -1
- decay_log: bfloat16 [32], P('dp'), may hold values from -4 to 0
- skip_gain: bfloat16 [32], P('dp'), may hold values from 0.5 to 1.5
Outputs:
- mixed: bfloat16 [8, 2048, 1024], P('dp', 'seq')
- grad_tokens: bfloat16 [8, 2048, 1024], P('dp', 'seq')
- grad_in_weight: float32 [1024, 4384], P('dp')
- grad_out_weight: float32 [2048, 1024], P('dp')
- grad_conv_weight: float32 [4, 2304], P(None, 'dp')
- grad_conv_bias: float32 [2304], P('dp')
- grad_pre_gain: float32 [1024], P('dp')
- grad_norm_gain: float32 [2048], P('dp')
- grad_step_bias: float32 [32], P('dp')
- grad_decay_log: float32 [32], P('dp')
- grad_skip_gain: float32 [32], P('dp')
All inputs are finite; a program needn't handle non-finite values.
Results may differ from a plain program's by a relative error of at most 0.017.
Values may be sent and summed in bfloat16 or wider, within the bound.
No kernel may reach another device: no remote copies, remote signals or barrier semaphores. Data moves between devices by JAX's collectives and lax.ppermute only.
A program may use at most 192 MiB of HBM per device.

v0:
```python
import jax
import jax.numpy as jnp
from jax import lax
from jax.sharding import PartitionSpec as P

HEADS = 32
HEAD_DIM = 64
STATE = 128
CONV = 4
GROUP = 256
INNER = 2048
CONV_CH = 2304


epsilon = 1e-05


def passed_along(block, axis, distance):
    devices = range(lax.axis_size(axis))
    route = [(i - distance, i) for i in devices if i - distance in devices]
    return lax.ppermute(block, axis, route)


def prefix_2(array, axis, join, neutral):
    place = lax.axis_index(axis)
    gathered = jax.tree.map(
        lambda a, kind: lax.all_gather(a.astype(kind), axis), array, (jnp.bfloat16, jnp.bfloat16)
    )
    state = jax.tree.map(lambda a, e: jnp.zeros_like(a) + jnp.asarray(e, a.dtype), array, neutral)

    def one(lap, state):
        return join(
            state,
            jax.tree.map(
                lambda a, own: lax.dynamic_index_in_dim(a, lap, 0, False).astype(own.dtype),
                gathered,
                array,
            ),
        )

    return lax.fori_loop(0, place, one, state)


def carried_in(array, axis, combine, identity):
    length, here = (lax.axis_size(axis), lax.axis_index(axis))
    everything = jax.tree.map(
        lambda part, kind: lax.all_gather(part.astype(kind), axis),
        array,
        jax.tree.map(lambda a: jnp.bfloat16 if a.dtype == jnp.float32 else a.dtype, array),
    )
    start = jax.tree.map(
        lambda part, zero: jnp.broadcast_to(jnp.asarray(zero, part.dtype), part.shape),
        array,
        identity,
    )

    def lap(k, before):
        at = length - 1 - k
        reached = at > here
        new = combine(
            before, jax.tree.map(lambda part, own: part[at].astype(own.dtype), everything, array)
        )
        return jax.tree.map(lambda a, b: jnp.where(reached, a, b), new, before)

    return lax.fori_loop(0, length, lap, start)


def rms_scale(values, gains):
    return values * lax.rsqrt(jnp.mean(values * values, axis=-1, keepdims=True) + epsilon) * gains


def group_part(log_decays, weighted, keys, queries):
    cumul = jnp.cumsum(log_decays, axis=0)
    places = jnp.arange(cumul.shape[0])
    causal = (places[:, None] >= places[None, :])[:, :, None]
    gaps = jnp.where(causal, cumul[:, None, :] - cumul[None, :, :], 0.0)
    kernel = jnp.where(causal, jnp.exp(gaps), 0.0)
    intersection = jnp.dot(queries, keys.T, precision=lax.Precision.HIGHEST)
    intra = jnp.einsum(
        "tsh,shp->thp", kernel * intersection[:, :, None], weighted, precision=lax.Precision.HIGHEST
    )
    tails = jnp.exp(cumul[-1][None, :] - cumul)
    block_state = jnp.einsum(
        "sh,shp,sn->hpn", tails, weighted, keys, precision=lax.Precision.HIGHEST
    )
    return (intra, block_state, cumul)


def front_piece(projected, before, conv_taps, conv_shift, bias_step, log_rates):
    length = projected.shape[0]
    gate_part = projected[:, :INNER]
    conv_in = jnp.concatenate([before, projected[:, INNER : INNER + CONV_CH]], axis=0)
    step_raw = projected[:, INNER + CONV_CH :]
    conv_out = conv_shift + sum((conv_in[k : k + length] * conv_taps[k] for k in range(CONV)))
    conv_act = jax.nn.silu(conv_out)
    heads_x = conv_act[:, :INNER].reshape(length, HEADS, HEAD_DIM)
    keys = conv_act[:, INNER : INNER + STATE]
    queries = conv_act[:, INNER + STATE :]
    step_size = jax.nn.softplus(step_raw + bias_step)
    log_decays = -step_size * jnp.exp(log_rates)
    weighted = heads_x * step_size[:, :, None]
    count = length // GROUP
    query_blocks = queries.reshape(count, GROUP, STATE)
    intra, block_states, cumuls = jax.vmap(group_part)(
        log_decays.reshape(count, GROUP, HEADS),
        weighted.reshape(count, GROUP, HEADS, HEAD_DIM),
        keys.reshape(count, GROUP, STATE),
        query_blocks,
    )
    device_state = jnp.zeros_like(block_states[0])
    for index in range(count):
        device_state = (
            jnp.exp(cumuls[index, -1])[:, None, None] * device_state + block_states[index]
        )
    device_decay = jnp.exp(jnp.sum(log_decays, axis=0))
    carried = (gate_part, heads_x, query_blocks, cumuls, block_states, intra)
    return ((device_decay, device_state), carried)


def back_piece(carried, start_state, gains_norm, skip_full):
    gate_part, heads_x, query_blocks, cumuls, block_states, intra = carried
    count = cumuls.shape[0]
    listed = []
    current = start_state
    for index in range(count):
        listed.append(current)
        current = jnp.exp(cumuls[index, -1])[:, None, None] * current + block_states[index]
    starts = jnp.stack(listed)
    inter = (
        jnp.einsum("cqn,chpn->cqhp", query_blocks, starts, precision=lax.Precision.HIGHEST)
        * jnp.exp(cumuls)[:, :, :, None]
    )
    length = heads_x.shape[0]
    ssm_out = (intra + inter).reshape(length, HEADS, HEAD_DIM) + skip_full[:, None] * heads_x
    gated = ssm_out.reshape(length, INNER) * jax.nn.silu(gate_part)
    return rms_scale(gated, gains_norm)


def combine(earlier, later):
    return (earlier[0] * later[0], later[0][:, None, None] * earlier[1] + later[1])


def shards(
    tokens,
    cotangent,
    in_weight,
    out_weight,
    conv_weight,
    conv_bias,
    pre_gain,
    norm_gain,
    step_bias,
    decay_log,
    skip_gain,
):
    gathered = (
        lax.all_gather(in_weight, "dp", axis=0, tiled=True),
        lax.all_gather(out_weight, "dp", axis=0, tiled=True),
        lax.all_gather(conv_weight, "dp", axis=1, tiled=True),
        lax.all_gather(conv_bias, "dp", axis=0, tiled=True),
        lax.all_gather(pre_gain, "dp", axis=0, tiled=True),
        lax.all_gather(norm_gain, "dp", axis=0, tiled=True),
        lax.all_gather(step_bias, "dp", axis=0, tiled=True),
        lax.all_gather(decay_log, "dp", axis=0, tiled=True),
        lax.all_gather(skip_gain, "dp", axis=0, tiled=True),
    )
    full_in = gathered[0]
    full_out = gathered[1]
    conv_taps, conv_shift, gains_pre, gains_norm, bias_step, log_rates, skip_full = [
        piece.astype(jnp.float32) for piece in gathered[2:]
    ]
    rows = tokens[0].astype(jnp.float32)
    length = rows.shape[0]
    normed_full, pre_pull = jax.vjp(rms_scale, rows, gains_pre)
    normed = normed_full.astype(jnp.bfloat16)
    projected = jnp.dot(normed, full_in, preferred_element_type=jnp.float32)
    edge = projected[length - (CONV - 1) :, INNER : INNER + CONV_CH]
    before = passed_along(edge, "seq", 1)
    front_out, front_pull = jax.vjp(
        front_piece, projected, before, conv_taps, conv_shift, bias_step, log_rates
    )
    summary, carried = front_out
    identity = (jnp.ones_like(summary[0]), jnp.zeros_like(summary[1]))
    prefix = prefix_2((summary[0], summary[1]), "seq", combine, identity)
    start_state = prefix[1]
    normed_out_full, back_pull = jax.vjp(back_piece, carried, start_state, gains_norm, skip_full)
    normed_out = normed_out_full.astype(jnp.bfloat16)
    mixed = (rows + jnp.dot(normed_out, full_out, preferred_element_type=jnp.float32)).astype(
        jnp.bfloat16
    )
    back_in, back_out = (
        lax.all_gather(in_weight, "dp", axis=0, tiled=True),
        lax.all_gather(out_weight, "dp", axis=0, tiled=True),
    )
    cot_rows = cotangent[0]
    grad_out_full = lax.dot_general(
        normed_out, cot_rows, (((0,), (0,)), ((), ())), preferred_element_type=jnp.float32
    )
    grad_normed_out = lax.dot_general(
        cot_rows, back_out, (((1,), (1,)), ((), ())), preferred_element_type=jnp.float32
    )
    grad_carried, grad_start, grad_gains_norm, grad_skip = back_pull(grad_normed_out)
    later = carried_in((summary[0], grad_start), "seq", combine, identity)
    grad_state = later[1]
    grad_decay_device = jnp.sum(grad_state * start_state, axis=(1, 2))
    grad_projected, grad_before, grad_taps, grad_shift, grad_bias_step, grad_rates = front_pull(
        ((grad_decay_device, grad_state), grad_carried)
    )
    returned = passed_along(grad_before, "seq", -1)
    grad_projected = (
        grad_projected.at[length - (CONV - 1) :, INNER : INNER + CONV_CH]
        .add(returned)
        .astype(jnp.bfloat16)
    )
    grad_in_full = lax.dot_general(
        normed, grad_projected, (((0,), (0,)), ((), ())), preferred_element_type=jnp.float32
    )
    grad_normed = lax.dot_general(
        grad_projected, back_in, (((1,), (1,)), ((), ())), preferred_element_type=jnp.float32
    )
    grad_rows, grad_gains_pre = pre_pull(grad_normed)
    grad_tokens = (cot_rows.astype(jnp.float32) + grad_rows).astype(jnp.bfloat16)
    shares = (
        lax.psum_scatter(
            grad_in_full.astype(jnp.bfloat16), "dp", scatter_dimension=0, tiled=True
        ).astype(jnp.float32),
        lax.psum_scatter(
            grad_out_full.astype(jnp.bfloat16), "dp", scatter_dimension=0, tiled=True
        ).astype(jnp.float32),
        lax.psum_scatter(
            grad_taps.astype(jnp.bfloat16), "dp", scatter_dimension=1, tiled=True
        ).astype(jnp.float32),
        lax.psum_scatter(
            grad_shift.astype(jnp.bfloat16), "dp", scatter_dimension=0, tiled=True
        ).astype(jnp.float32),
        lax.psum_scatter(
            grad_gains_pre.astype(jnp.bfloat16), "dp", scatter_dimension=0, tiled=True
        ).astype(jnp.float32),
        lax.psum_scatter(
            grad_gains_norm.astype(jnp.bfloat16), "dp", scatter_dimension=0, tiled=True
        ).astype(jnp.float32),
        lax.psum_scatter(
            grad_bias_step.astype(jnp.bfloat16), "dp", scatter_dimension=0, tiled=True
        ).astype(jnp.float32),
        lax.psum_scatter(
            grad_rates.astype(jnp.bfloat16), "dp", scatter_dimension=0, tiled=True
        ).astype(jnp.float32),
        lax.psum_scatter(
            grad_skip.astype(jnp.bfloat16), "dp", scatter_dimension=0, tiled=True
        ).astype(jnp.float32),
    )
    totals = (
        lax.psum(shares[0].astype(jnp.bfloat16), "seq").astype(jnp.float32),
        lax.psum(shares[1].astype(jnp.bfloat16), "seq").astype(jnp.float32),
        lax.psum(shares[2].astype(jnp.bfloat16), "seq").astype(jnp.float32),
        lax.psum(shares[3].astype(jnp.bfloat16), "seq").astype(jnp.float32),
        lax.psum(shares[4].astype(jnp.bfloat16), "seq").astype(jnp.float32),
        lax.psum(shares[5].astype(jnp.bfloat16), "seq").astype(jnp.float32),
        lax.psum(shares[6].astype(jnp.bfloat16), "seq").astype(jnp.float32),
        lax.psum(shares[7].astype(jnp.bfloat16), "seq").astype(jnp.float32),
        lax.psum(shares[8].astype(jnp.bfloat16), "seq").astype(jnp.float32),
    )
    return (
        mixed[None],
        grad_tokens[None],
        totals[0],
        totals[1],
        totals[2],
        totals[3],
        totals[4],
        totals[5],
        totals[6],
        totals[7],
        totals[8],
    )


def solution(mesh):
    return jax.shard_map(
        shards,
        mesh=mesh,
        in_specs=(
            P("dp", "seq", None),
            P("dp", "seq", None),
            P("dp", None),
            P("dp", None),
            P(None, "dp"),
            P("dp"),
            P("dp"),
            P("dp"),
            P("dp"),
            P("dp"),
            P("dp"),
        ),
        out_specs=(
            P("dp", "seq", None),
            P("dp", "seq", None),
            P("dp", None),
            P("dp", None),
            P(None, "dp"),
            P("dp"),
            P("dp"),
            P("dp"),
            P("dp"),
            P("dp"),
            P("dp"),
        ),
        check_vma=False,
    )
```

profile of v0, /device:TPU:0, one launch (start us, length us, event | category | flops | bytes accessed | tf_op | source)
XLA Modules:
  0.0 884.8 jit_solution(7286519971055459142)
XLA Ops:
  10.6 22.5 %all-gather.1 = bf16[8,1,128]{2,1,0:T(2,128)(2,1)S(1)} all-gather(bf16[1,1,128]{2,1,0:T(2,128)(2,1)} %bitcast.270), channel_id=1, replica_groups=mesh['dp'=8,'seq'=4] {'dp'}, dimensions={0}, use_global_device_ids=true | all-gather | bytes 2304 | tf_op jit(solution)/shard_map/all_gather | solution.py:161
  36.5 18.6 %all-reduce.33 = (bf16[2304]{0:T(1024)(128)(2,1)S(1)}, bf16[32]{0:T(256)(128)(2,1)S(1)}, bf16[32]{0:T(256)(128)(2,1)S(1)}, bf16[32]{0:T(256)(128)(2,1)}) all-reduce(bf16[2304]{0:T(1024)(128)(2,1)S(1)} %dynamic-update-slice.2, bf16[32]{0:T(256)(128)(2,1)S(1)} %dynamic-update-slice.3, ...), channel_id=1, replica_groups=mesh['dp'=8,'seq'=4] {'dp'}, use_global_device_ids=true, to_apply=%add.21 | all-reduce | flops 2400 | bytes 9600
  55.1 43.0 %all-gather.2 = bf16[8,288,4]{1,2,0:T(4,128)(2,1)S(1)} all-gather(bf16[1,288,4]{1,2,0:T(4,128)(2,1)} %bitcast.266), channel_id=1, replica_groups=mesh['dp'=8,'seq'=4] {'dp'}, dimensions={0}, use_global_device_ids=true | all-gather | bytes 20736 | tf_op jit(solution)/shard_map/all_gather | solution.py:159
  98.3 1.5 fusion.56
  99.9 46.3 %all-gather.9.cloned.1.call-done = bf16[1024,4384]{0,1:T(8,128)(2,1)} async-done(((bf16[128,4384]{0,1:T(8,128)(2,1)}), bf16[1024,4384]{0,1:T(8,128)(2,1)}) %all-gather.9.cloned.1.call-update) | async-done | bytes 8978448 | tf_op jit(solution)/shard_map/all_gather | solution.py:157
  146.2 8.0 fusion.95
  154.3 3.5 copy-done.5
  160.3 1.6 slice.120
  164.5 5.0 slice.121
  170.0 13.8 %fusion.27 = (f32[512,2304]{0,1:T(8,128)S(1)}, f32[512,2304]{0,1:T(8,128)}) fusion(f32[512,2304]{0,1:T(8,128)} %slice.121, f32[2304]{0:T(1024)S(1)} %get-tuple-element.238, f32[2304]{0:T(1024)S(1)} %get-tuple-element.239, f32[3,2304]{0,1:T(8,128)S(1)} %copy.185, f32[2304]{0:T(1024)S(1)} %get-tuple-element.240, f32[2304]{0:T(1024)S(1)} %get-tuple-element.237, ...), kind=kLoop, calls=%fused_computation.48 | loop fusion | flops 17694720 | bytes 14229504 | tf_op jit(solution)/shard_map/jvp(jit(silu))/mul | solution.py:95
  183.9 3.0 slice.130
  187.7 5.9 reshape.287
  193.6 6.1 fusion.41
  202.4 18.3 %all-gather.3 = bf16[8,1,256]{2,1,0:T(2,128)(2,1)S(1)} all-gather(bf16[1,1,256]{2,1,0:T(2,128)(2,1)S(1)} %reshape.333), channel_id=1, replica_groups=mesh['dp'=8,'seq'=4] {'dp'}, dimensions={0}, use_global_device_ids=true | all-gather | bytes 4608 | tf_op jit(solution)/shard_map/all_gather | solution.py:162
  222.5 5.6 all-reduce.24
  230.1 1.4 fusion.123
  233.5 4.7 fusion.74
  238.3 2.1 copy-done.10
  240.4 19.5 %bitcast_add_fusion.1 = f32[2,256,32,64]{1,3,2,0:T(8,128)S(1)} fusion(f32[2,256,32,64]{1,3,2,0:T(8,128)S(1)} %fusion.74, f32[2,256,32]{1,2,0:T(8,128)S(1)} %copy-done.32, f32[2,256,256]{2,1,0:T(8,128)S(1)} %copy-done.35, f32[2,256,32]{1,2,0:T(8,128)S(1)} %copy-done.39, pred[256,256]{1,0:T(8,128)(4,1)S(1)} %copy-done.52, ...), kind=kOutput, calls=%fused_computation.58 | convolution fusion | flops 3241148416 | bytes 13369344 | tf_op jit(solution)/shard_map/jvp(vmap(tsh,shp->thp))/dot_general | solution.py:79
  259.8 3.4 copy.196
  263.7 3.2 slice-done.1
  267.0 4.6 multiply_reduce_fusion.10
  271.6 26.8 %all-gather.13.cloned.1.call-done = bf16[2048,1024]{1,0:T(8,128)(2,1)} async-done(((bf16[256,1024]{1,0:T(8,128)(2,1)}), bf16[2048,1024]{1,0:T(8,128)(2,1)}) %all-gather.13.cloned.1.call-update) | async-done | bytes 4194320 | tf_op jit(solution)/shard_map/all_gather | solution.py:158
  298.4 7.2 multiply_reduce_fusion.6
  305.7 19.4 %multiply_reduce_fusion.5 = (f32[2048]{0:T(1024)S(1)}, f32[512,2048]{0,1:T(8,128)}, f32[512,2048]{0,1:T(8,128)}) fusion(f32[512,2304]{0,1:T(8,128)} %copy-done, f32[512,4384]{0,1:T(8,128)} %copy-done.5, f32[512,2048]{0,1:T(8,128)S(1)} %copy-done.11, f32[512]{0:T(512)S(1)} %multiply_multiply_fusion.1, f32[512]{0:T(512)S(1)} %fusion.106, ...), kind=kLoop, calls=%fused_computation.66 | loop fusion | flops 22018048 | bytes 29388800 | tf_op jit(solution)/shard_map/transpose(jvp())/reduce_sum | solution.py:134
  325.1 5.9 reshape.295
  331.0 6.1 fusion.37
  339.9 8.9 %fusion.79 = f32[2,256,128]{2,1,0:T(8,128)S(1)} fusion(f32[1,32,64,128]{3,2,1,0:T(8,128)S(1)} %copy-done.17, f32[1,32,64,128]{3,2,1,0:T(8,128)S(1)} %bitcast.224, f32[2,256,32,64]{1,0,3,2:T(2,128)} %reshape.295, f32[2,256,32]{1,2,0:T(8,128)} %get-tuple-element.306), kind=kOutput, calls=%fused_computation.124 | convolution fusion | flops 1612185600 | bytes 6619136 | tf_op jit(solution)/shard_map/transpose(jvp(cqn,chpn->cqhp))/dot_general | solution.py:130
  348.8 26.8 %fusion.12 = (f32[2,256,32]{1,2,0:T(8,128)}, f32[2,256,32]{1,2,0:T(8,128)}, f32[2,256,256]{2,1,0:T(8,128)S(1)}) fusion(f32[2,256,256]{2,1,0:T(8,128)S(1)} %copy-done.36, f32[2,256,32]{1,2,0:T(8,128)S(1)} %copy-done.40, pred[256,256]{1,0:T(8,128)(4,1)S(1)} %copy-done.53, f32[2,256,32,64]{1,0,3,2:T(2,128)S(1)} %copy-done.2, f32[2,256,32]{1,2,0:T(8,128)S(1)} %bitcast.247, ...), kind=kOutput, calls=%fused_computation.17 | convolution fusion | flops 3268247552 | bytes 9764864 | tf_op jit(solution)/shard_map/transpose(jvp(vmap(tsh,shp->thp)))/dot_general | solution.py:79
  377.1 5.0 multiply_reduce_fusion.7
  382.1 5.8 while.30
  387.9 3.1 multiply_reduce_fusion.12
  391.0 6.8 fusion.76
  397.9 4.6 multiply_reduce_fusion.4
  403.8 15.6 %bitcast_add_fusion = f32[2,256,32,64]{1,3,2,0:T(8,128)} fusion(f32[2,256,32,64]{1,3,2,0:T(8,128)S(1)} %get-tuple-element.312, f32[2,256,32]{1,2,0:T(8,128)S(1)} %copy-done.31, f32[2,256,256]{2,1,0:T(8,128)S(1)} %copy-done.37, f32[2,256,32]{1,2,0:T(8,128)S(1)} %copy-done.41, pred[256,256]{1,0:T(8,128)(4,1)S(1)} %copy-done.54, ...), kind=kOutput, calls=%fused_computation.54 | convolution fusion | flops 3240099840 | bytes 13303808 | tf_op jit(solution)/shard_map/transpose(jvp(vmap(tsh,shp->thp)))/dot_general | solution.py:79
  419.5 5.7 copy.202
  425.7 2.8 fusion.30
  428.5 1.6 slice-done.4
  432.1 9.8 %multiply_reduce_fusion.2 = (f32[2304]{0:T(1024)S(1)}, f32[2304]{0:T(1024)S(1)}, f32[2304]{0:T(1024)S(1)}, bf16[2304]{0:T(1024)(128)(2,1)S(1)}, f32[2304]{0:T(1024)S(1)}, /*index=5*/f32[512,2304]{0,1:T(8,128)S(1)}) fusion(f32[512,2304]{0,1:T(8,128)S(1)} %bitcast.230, f32[3,2304]{0,1:T(8,128)S(1)} %copy-done.14, f32[512,4384]{0,1:T(8,128)S(1)} %bitcast.232, ...), kind=kLoop, calls=%fused_computation.45 | loop fusion | flops 27120384 | bytes 23662080 | tf_op jit(solution)/shard_map/transpose(jvp())/reduce_sum | solution.py:94
  441.9 1.8 broadcast_multiply_fusion
  444.5 7.0 pad_add_fusion.1
  452.3 5.0 reduce-window.16
  457.6 2.9 copy.251
  460.5 3.5 multiply_reduce_fusion.8
  464.0 3.5 split.8
  469.2 1.6 fusion.115
  470.7 6.2 pad_add_fusion
  477.4 1.6 slice_add_fusion
  479.0 7.8 scatter-add.4
  486.8 11.1 %convolution_convert_fusion = bf16[1024,4384]{0,1:T(8,128)(2,1)} fusion(f32[512,4384]{0,1:T(8,128)} %scatter-add.4, bf16[1,512,1024]{2,1,0:T(8,128)(2,1)S(1)} %copy-done.15, f32[1024]{0:T(1024)S(1)} %bitcast.258, f32[512]{0:T(512)S(1)} %copy-done.64), kind=kOutput, calls=%fused_computation.18 | convolution fusion | flops 4605788160 | bytes 19011584 | tf_op jit(solution)/shard_map/dot_general | solution.py:215
  497.9 12.0 %copy.242 = bf16[1024,4384]{1,0:T(8,128)(2,1)} copy(bf16[1024,4384]{0,1:T(8,128)(2,1)} %convolution_convert_fusion) | data formatting | bytes 17956864
  511.2 6.6 convolution_convert_fusion.1
  520.7 6.9 fusion.75
  528.9 140.3 %reduce-scatter.10.cloned.1.call-done = bf16[128,4384]{1,0:T(8,128)(2,1)} async-done(((bf16[1024,4384]{1,0:T(8,128)(2,1)}), bf16[128,4384]{1,0:T(8,128)(2,1)}) %reduce-scatter.10.cloned.1.call-update) | async-done | bytes 1122320
  669.2 2.4 copy.243
  671.5 88.6 %reduce-scatter.8.cloned.1.call-done = bf16[256,1024]{1,0:T(8,128)(2,1)} async-done(((bf16[2048,1024]{1,0:T(8,128)(2,1)}), bf16[256,1024]{1,0:T(8,128)(2,1)}) %reduce-scatter.8.cloned.1.call-update) | async-done | bytes 524304 | tf_op jit(solution)/shard_map/reduce_scatter | solution.py:227
  760.1 10.5 %fusion.53 = (bf16[1024]{0:T(1024)(128)(2,1)S(1)}, f32[512]{0:T(512)S(1)}, f32[512,1024]{1,0:T(8,128)S(1)}) fusion(bf16[1,512,1024]{2,1,0:T(8,128)(2,1)S(1)} %copy-done.15, f32[512]{0:T(512)S(1)} %copy-done.64, f32[1024]{0:T(1024)S(1)} %bitcast.259, bf16[1024,4384]{0,1:T(8,128)(2,1)} %all-gather.9.cloned.1.call-done, f32[512,4384]{0,1:T(8,128)} %scatter-add.4), kind=kOutput, calls=%fused_computation.100 | convolution fusion | flops 4602870272 | bytes 21112832 | tf_op jit(solution)/shard_map/dot_general | solution.py:218
  770.7 36.0 %all-reduce.32 = (bf16[2304]{0:T(1024)(128)(2,1)S(1)}, bf16[1024]{0:T(1024)(128)(2,1)S(1)}, bf16[2048]{0:T(1024)(128)(2,1)S(1)}, bf16[32]{0:T(256)(128)(2,1)S(1)...) all-reduce(bf16[2304]{0:T(1024)(128)(2,1)S(1)} %get-tuple-element.2, ...), channel_id=6, replica_groups=mesh['dp'=8,'seq'=4] {'dp'}, use_global_device_ids=true, to_apply=%region_34.35.clone | all-reduce | flops 5472 | bytes 21888
  807.2 2.8 fusion.82
  810.0 15.8 %reduce-scatter.12.cloned.1.call-done = bf16[288,4]{1,0:T(8,128)(2,1)} async-done(((bf16[2304,4]{1,0:T(8,128)(2,1)}), bf16[288,4]{1,0:T(8,128)(2,1)}) %reduce-scatter.12.cloned.1.call-update) | async-done | bytes 2320
  826.8 5.8 all-reduce.34
  836.4 36.2 %all-reduce.38.cloned.1.call-done = (bf16[128,4384]{0,1:T(8,128)(2,1)}, bf16[256,1024]{1,0:T(8,128)(2,1)}) async-done(((bf16[128,4384]{0,1:T(8,128)(2,1)}, bf16[256,1024]{1,0:T(8,128)(2,1)}), (bf16[128,4384]{0,1:T(8,128)(2,1)}, bf16[256,1024]{1,0:T(8,128)(2,1)})) %all-reduce.38.cloned.1.call-update) | async-done | bytes 1646608 | tf_op jit(solution)/shard_map/psum | solution.py:253
  872.6 2.1 convert_element_type.209
  874.7 2.8 convert_element_type.207
  (342 shorter events, 45.1 us)
Async XLA Ops:
  7.2 139.0 %all-gather.9.cloned.1.call-start = ((), (), s32[]{:S(2)}) async-start(), calls=%async_computation.3 | async-start | bytes 10100736 | tf_op jit(solution)/shard_map/all_gather | solution.py:157
  7.9 223.5 %all-gather.11.cloned.1.call-start = ((), (), s32[]{:S(2)}) async-start(), calls=%async_computation.4 | async-start | bytes 2621440 | tf_op jit(solution)/shard_map/all_gather | solution.py:27
  33.0 121.1 %copy-start.59 = (f32[8,1,128]{2,1,0:T(1,128)}, f32[8,1,128]{2,1,0:T(1,128)S(1)}, u32[]{:S(2)}) copy-start(f32[8,1,128]{2,1,0:T(1,128)S(1)} %convert_element_type.229) | copy-start | bytes 12292
  55.1 99.1 %copy-start.92 = (bf16[32]{0:T(256)(128)(2,1)}, bf16[32]{0:T(256)(128)(2,1)S(1)}, u32[]{:S(2)}) copy-start(bf16[32]{0:T(256)(128)(2,1)S(1)} %get-tuple-element.269) | copy-start | bytes 196
  55.1 99.1 %copy-start.76 = (f32[32]{0:T(128)}, f32[32]{0:T(128)S(1)}, u32[]{:S(2)}) copy-start(f32[32]{0:T(128)S(1)} %convert_element_type.193) | copy-start | bytes 388
  98.3 71.7 %copy-start.44 = (f32[2304]{0:T(1024)}, f32[2304]{0:T(1024)S(1)}, u32[]{:S(2)}) copy-start(f32[2304]{0:T(1024)S(1)} %get-tuple-element.237) | copy-start | bytes 27652
  98.3 71.7 %copy-start.46 = (f32[2304]{0:T(1024)}, f32[2304]{0:T(1024)S(1)}, u32[]{:S(2)}) copy-start(f32[2304]{0:T(1024)S(1)} %get-tuple-element.238) | copy-start | bytes 27652
  98.3 71.7 %copy-start.48 = (f32[2304]{0:T(1024)}, f32[2304]{0:T(1024)S(1)}, u32[]{:S(2)}) copy-start(f32[2304]{0:T(1024)S(1)} %get-tuple-element.239) | copy-start | bytes 27652
  98.3 71.7 %copy-start.50 = (f32[2304]{0:T(1024)}, f32[2304]{0:T(1024)S(1)}, u32[]{:S(2)}) copy-start(f32[2304]{0:T(1024)S(1)} %get-tuple-element.240) | copy-start | bytes 27652
  99.9 54.4 %copy-start.65 = (f32[512]{0:T(512)}, f32[512]{0:T(512)S(1)}, u32[]{:S(2)}) copy-start(f32[512]{0:T(512)S(1)} %fusion.56) | copy-start | bytes 6148
  99.9 54.4 %copy-start.78 = (f32[32]{0:T(128)}, f32[32]{0:T(128)S(1)}, u32[]{:S(2)}) copy-start(f32[32]{0:T(128)S(1)} %convert_exponential_fusion) | copy-start | bytes 388
  99.9 54.3 %copy-start.63 = (f32[512]{0:T(512)}, f32[512]{0:T(512)S(1)}, u32[]{:S(2)}) copy-start(f32[512]{0:T(512)S(1)} %fusion.105) | copy-start | bytes 6148
  159.6 9.9 %copy-start.24 = (f32[2,32,2,128]{3,1,2,0:T(8,128)}, f32[2,32,2,128]{3,1,2,0:T(8,128)S(1)}, u32[]{:S(2)}) copy-start(f32[2,32,2,128]{3,1,2,0:T(8,128)S(1)} %reduce-window.14) | copy-start | bytes 196612
  159.9 9.7 %copy-start.57 = (f32[2,32,2]{1,2,0:T(2,128)}, f32[2,32,2]{1,2,0:T(2,128)S(1)}, u32[]{:S(2)}) copy-start(f32[2,32,2]{1,2,0:T(2,128)S(1)} %slice.133) | copy-start | bytes 1540
  160.0 9.6 %copy-start.38 = (f32[2,256,32]{1,2,0:T(8,128)}, f32[2,256,32]{1,2,0:T(8,128)S(1)}, u32[]{:S(2)}) copy-start(f32[2,256,32]{1,2,0:T(8,128)S(1)} %bitcast_bitcast_fusion.1) | copy-start | bytes 196612
  160.3 9.2 %copy-start.73 = (f32[32]{0:T(128)}, f32[32]{0:T(128)S(1)}, u32[]{:S(2)}) copy-start(f32[32]{0:T(128)S(1)} %get-tuple-element.236) | copy-start | bytes 388
  160.3 39.3 %copy-start.71 = (f32[32]{0:T(128)}, f32[32]{0:T(128)S(1)}, u32[]{:S(2)}) copy-start(f32[32]{0:T(128)S(1)} %get-tuple-element.235) | copy-start | bytes 388
  163.1 6.4 collective-permute-start
  164.5 35.2 %copy-start.81 = (f32[32]{0:T(128)}, f32[32]{0:T(128)S(1)}, u32[]{:S(2)}) copy-start(f32[32]{0:T(128)S(1)} %broadcast_multiply_fusion.4) | copy-start | bytes 388
  170.0 13.9 %copy-start.13 = (f32[3,2304]{0,1:T(8,128)}, f32[3,2304]{0,1:T(8,128)S(1)}, u32[]{:S(2)}) copy-start(f32[3,2304]{0,1:T(8,128)S(1)} %copy.185) | copy-start | bytes 82948
  193.6 8.2 copy-start.95
  193.6 8.8 copy-start.91
  193.6 27.2 %copy-start.89 = (bf16[32]{0:T(256)(128)(2,1)S(1)}, bf16[32]{0:T(256)(128)(2,1)}, u32[]{:S(2)}) copy-start(bf16[32]{0:T(256)(128)(2,1)} %get-tuple-element.270) | copy-start | bytes 196
  193.6 28.6 %copy-start.86 = (f32[32]{0:T(128)S(1)}, f32[32]{0:T(128)}, u32[]{:S(2)}) copy-start(f32[32]{0:T(128)} %get-tuple-element.287) | copy-start | bytes 388
  199.7 31.9 %copy-start.9 = (f32[2,32,64,128]{3,2,1,0:T(8,128)}, f32[2,32,64,128]{3,2,1,0:T(8,128)S(1)}, u32[]{:S(2)}) copy-start(f32[2,32,64,128]{3,2,1,0:T(8,128)S(1)} %fusion.41) | copy-start | bytes 6291460
  201.0 97.5 %all-gather.13.cloned.1.call-start = ((), (), s32[]{:S(2)}) async-start(), calls=%async_computation.5 | async-start | bytes 4718592 | tf_op jit(solution)/shard_map/all_gather | solution.py:158
  201.7 180.4 %all-gather.15.cloned.1.call-start = ((), (), s32[]{:S(2)}) async-start(), calls=%async_computation.6 | async-start | bytes 2621440 | tf_op jit(solution)/shard_map/all_gather | solution.py:47
  220.7 77.7 %copy-start.61 = (f32[8,1,256]{2,1,0:T(1,128)}, f32[8,1,256]{2,1,0:T(1,128)S(1)}, u32[]{:S(2)}) copy-start(f32[8,1,256]{2,1,0:T(1,128)S(1)} %convert_element_type.231) | copy-start | bytes 24580
  231.6 8.8 copy-start.1
  231.6 8.7 copy-start.32
  231.6 8.7 copy-start.35
  231.6 8.7 copy-start.39
  231.6 8.7 copy-start.52
  263.7 7.9 copy-start.7
  266.9 31.5 %copy-start.27 = (bf16[1,512,1024]{2,1,0:T(8,128)(2,1)S(1)}, bf16[1,512,1024]{2,1,0:T(8,128)(2,1)}, u32[]{:S(2)}) copy-start(bf16[1,512,1024]{2,1,0:T(8,128)(2,1)} %param.18) | copy-start | bytes 3145732
  271.6 34.1 %copy-start.69 = (f32[512]{0:T(512)}, f32[512]{0:T(512)S(1)}, u32[]{:S(2)}) copy-start(f32[512]{0:T(512)S(1)} %fusion.106) | copy-start | bytes 6148
  331.0 8.8 copy-start.17
  339.8 329.4 %reduce-scatter.10.cloned.1.call-start = ((), (), s32[]{:S(2)}) async-start(), calls=%async_computation.8 | async-start | bytes 10321920
  339.8 8.9 %copy-start.2 = (f32[2,256,32,64]{1,0,3,2:T(2,128)S(1)}, f32[2,256,32,64]{1,0,3,2:T(2,128)}, u32[]{:S(2)}) copy-start(f32[2,256,32,64]{1,0,3,2:T(2,128)} %reshape.287) | copy-start | bytes 12582916
  339.9 8.9 %copy-start.36 = (f32[2,256,256]{2,1,0:T(8,128)S(1)}, f32[2,256,256]{2,1,0:T(8,128)}, u32[]{:S(2)}) copy-start(f32[2,256,256]{2,1,0:T(8,128)} %fusion.123) | copy-start | bytes 1572868
  339.9 8.9 %copy-start.40 = (f32[2,256,32]{1,2,0:T(8,128)S(1)}, f32[2,256,32]{1,2,0:T(8,128)}, u32[]{:S(2)}) copy-start(f32[2,256,32]{1,2,0:T(8,128)} %copy-done.38) | copy-start | bytes 196612
  339.9 8.9 %copy-start.53 = (pred[256,256]{1,0:T(8,128)(4,1)S(1)}, pred[256,256]{1,0:T(8,128)(4,1)}, u32[]{:S(2)}) copy-start(pred[256,256]{1,0:T(8,128)(4,1)} %iota_compare_fusion) | copy-start | bytes 196612
  348.8 26.8 %copy-start.23 = (f32[2,256,128]{2,1,0:T(8,128)S(1)}, f32[2,256,128]{2,1,0:T(8,128)}, u32[]{:S(2)}) copy-start(f32[2,256,128]{2,1,0:T(8,128)} %copy-done.22) | copy-start | bytes 786436
  382.1 9.0 %copy-start.30 = (f32[2,256,32]{1,2,0:T(8,128)S(1)}, f32[2,256,32]{1,2,0:T(8,128)}, u32[]{:S(2)}) copy-start(f32[2,256,32]{1,2,0:T(8,128)} %get-tuple-element.307) | copy-start | bytes 196612
  432.0 9.8 %copy-start.45 = (f32[2304]{0:T(1024)S(1)}, f32[2304]{0:T(1024)}, u32[]{:S(2)}) copy-start(f32[2304]{0:T(1024)} %copy-done.44) | copy-start | bytes 27652
  432.0 9.8 %copy-start.47 = (f32[2304]{0:T(1024)S(1)}, f32[2304]{0:T(1024)}, u32[]{:S(2)}) copy-start(f32[2304]{0:T(1024)} %copy-done.46) | copy-start | bytes 27652
  432.0 9.8 %copy-start.49 = (f32[2304]{0:T(1024)S(1)}, f32[2304]{0:T(1024)}, u32[]{:S(2)}) copy-start(f32[2304]{0:T(1024)} %copy-done.48) | copy-start | bytes 27652
  432.0 9.8 %copy-start.51 = (f32[2304]{0:T(1024)S(1)}, f32[2304]{0:T(1024)}, u32[]{:S(2)}) copy-start(f32[2304]{0:T(1024)} %copy-done.50) | copy-start | bytes 27652
  444.4 7.7 copy-start.42
  444.4 7.8 copy-start.43
  444.4 7.8 copy-start.55
  444.4 7.8 copy-start.56
  467.8 9.1 %collective-permute-start.1 = (f32[3,2304]{1,0:T(4,128)S(1)}, f32[3,2304]{1,0:T(4,128)S(1)}, u32[]{:S(2)}, u32[]{:S(2)}) collective-permute-start(f32[3,2304]{1,0:T(4,128)S(1)} %copy.217), channel_id=1, source_target_pairs={{1,0},{2,1},{3,2},{5,4},{6,5},{7,6},{9,8},{10,9},{11,10},{13,12},{... | collective-permute-start | bytes 82952 | tf_op jit(solution)/shard_map/ppermute | solution.py:21
  476.9 9.9 %copy-start.15 = (bf16[1,512,1024]{2,1,0:T(8,128)(2,1)S(1)}, bf16[1,512,1024]{2,1,0:T(8,128)(2,1)}, u32[]{:S(2)}) copy-start(bf16[1,512,1024]{2,1,0:T(8,128)(2,1)} %param.17) | copy-start | bytes 3145732
  476.9 9.9 %copy-start.60 = (f32[8,1,128]{2,1,0:T(1,128)S(1)}, f32[8,1,128]{2,1,0:T(1,128)}, u32[]{:S(2)}) copy-start(f32[8,1,128]{2,1,0:T(1,128)} %copy-done.59) | copy-start | bytes 12292
  476.9 9.9 %copy-start.64 = (f32[512]{0:T(512)S(1)}, f32[512]{0:T(512)}, u32[]{:S(2)}) copy-start(f32[512]{0:T(512)} %copy-done.63) | copy-start | bytes 6148
  510.0 250.1 %reduce-scatter.8.cloned.1.call-start = ((), (), s32[]{:S(2)}) async-start(), calls=%async_computation.7 | async-start | bytes 4718592 | tf_op jit(solution)/shard_map/reduce_scatter | solution.py:227
  517.8 308.0 %reduce-scatter.12.cloned.1.call-start = ((), (), s32[]{:S(2)}) async-start(), calls=%async_computation.9 | async-start | bytes 663552
  520.7 8.2 copy-start.88
  520.7 8.2 copy-start.93
  528.8 343.8 %all-reduce.38.cloned.1.call-start = ((), (), s32[]{:S(2)}) async-start(), calls=%async_computation.10 | async-start | bytes 3293184 | tf_op jit(solution)/shard_map/psum | solution.py:253
  760.1 10.6 %copy-start.75 = (bf16[2048]{0:T(1024)(128)(2,1)S(1)}, bf16[2048]{0:T(1024)(128)(2,1)}, u32[]{:S(2)}) copy-start(bf16[2048]{0:T(1024)(128)(2,1)} %get-tuple-element.225) | copy-start | bytes 12292
  760.1 10.6 %copy-start.80 = (bf16[32]{0:T(256)(128)(2,1)S(1)}, bf16[32]{0:T(256)(128)(2,1)}, u32[]{:S(2)}) copy-start(bf16[32]{0:T(256)(128)(2,1)} %get-tuple-element.282) | copy-start | bytes 196
  760.1 47.0 %copy-start.66 = (f32[512]{0:T(512)S(1)}, f32[512]{0:T(512)}, u32[]{:S(2)}) copy-start(f32[512]{0:T(512)} %copy-done.65) | copy-start | bytes 6148
  (51 other events, 257.0 us)
Sparse Core Ops, SparseCore 0:
  10.1 136.0 all-gather.8
  201.1 21.7 all-gather.10
  225.0 73.3 all-gather.12
  339.9 20.8 all-gather.14
  510.1 159.0 reduce-scatter.9
  673.1 86.9 reduce-scatter.7
  763.9 61.8 reduce-scatter.11
  829.0 43.5 all-reduce.37
where the time goes:
time: 895 us; the launch traced here: 885 us
  waiting for transfers between devices  355 us (40%)
  matrix products  153 us (17%)
  blocking collectives  150 us (17%)
  other arithmetic  112 us (13%)
  local copies, waits for them, and re-layouts  90.7 us (10%)
  between operations  20.7 us (2%)
    unnamed x10, waiting for transfers between devices  157 us
    reduce_scatter x1, waiting for transfers between devices, shards(): lax.psum_scatter(grad_out_full.astype(jnp.bfloat16), 'dp', scatter_dimens...  88.6 us
    dot_general x3, matrix products, group_part(): jnp.einsum('tsh,shp->thp', kernel * intersection[:, :, None], weighted, p...  61.8 us
    unnamed x3, blocking collectives  60.2 us
    all_gather x1, waiting for transfers between devices, shards(): lax.all_gather(in_weight, 'dp', axis=0, tiled=True)  46.3 us
    all_gather x1, blocking collectives, shards(): lax.all_gather(conv_weight, 'dp', axis=1, tiled=True)  43 us
    unnamed x235, local copies, waits for them, and re-layouts  39.8 us
    psum x1, waiting for transfers between devices, shards(): lax.psum(shares[0].astype(jnp.bfloat16), 'seq').astype(jnp.float32)  36.2 us
  transfers between devices with their start and end apart: 10, of which 6 were waited for; matrix products, arithmetic and copies ran while one was open for 15% of the time, Pallas kernels for 0%

commit v1 on v0

v1 whole, which is shorter than its diff:
```python
import functools

import jax
import jax.numpy as jnp
from jax import lax
from jax.experimental import pallas as pl
from jax.experimental.pallas import tpu as pltpu
from jax.sharding import PartitionSpec as P

HEADS = 32
HEAD_DIM = 64
STATE = 128
CONV = 4
GROUP = 256
INNER = 2048
CONV_CH = 2304
EDGE = 16
TILE = 256
HPT = TILE // HEAD_DIM
TILES = INNER // TILE
LANES = 128

bf16 = jnp.bfloat16
f32 = jnp.float32
epsilon = 1e-05
VMEM_LIMIT = 40 * 1024 * 1024


def params(vmem=VMEM_LIMIT):
    return pltpu.CompilerParams(vmem_limit_bytes=vmem)


def mm(a, b, dims=((1,), (0,))):
    return lax.dot_general(a, b, (dims, ((), ())), preferred_element_type=f32)


NT = ((1,), (1,))
TN = ((0,), (0,))


def split3(v):
    hi = v.astype(bf16)
    rest = v - hi.astype(f32)
    mid = rest.astype(bf16)
    lo = (rest - mid.astype(f32)).astype(bf16)
    return hi, mid, lo


def split2(v):
    hi = v.astype(bf16)
    return hi, (v - hi.astype(f32)).astype(bf16)


def expander(tile):
    head = lax.broadcasted_iota(jnp.int32, (3 * HEADS, TILE), 0) % HEADS
    lane = lax.broadcasted_iota(jnp.int32, (3 * HEADS, TILE), 1)
    return (head == HPT * tile + lane // HEAD_DIM).astype(f32).astype(bf16)


def selector(tile):
    lane = lax.broadcasted_iota(jnp.int32, (TILE, LANES), 0)
    head = lax.broadcasted_iota(jnp.int32, (TILE, LANES), 1)
    return (head == HPT * tile + lane // HEAD_DIM).astype(f32).astype(bf16)


def head_sums(v, sel):
    hi, lo = split2(v)
    return mm(hi, sel) + mm(lo, sel)


def sigmoid(v):
    return 1.0 / (1.0 + jnp.exp(-v))


def conv_of(p_ref, taps_ref, shift_ref, length):
    out = shift_ref[0:1, :]
    for k in range(CONV):
        out = out + p_ref[pl.ds(EDGE - CONV + 1 + k, length), :] * taps_ref[k : k + 1, :]
    return out


def tri(lower):
    r = lax.broadcasted_iota(jnp.int32, (GROUP, GROUP), 0)
    c = lax.broadcasted_iota(jnp.int32, (GROUP, GROUP), 1)
    return ((r >= c) if lower else (r <= c)).astype(f32).astype(bf16)


def lasts(cum3_ref, blocks):
    return jnp.concatenate(
        [cum3_ref[(b + 1) * GROUP - 1 : (b + 1) * GROUP, :] for b in range(blocks)], axis=0
    )


def front_kernel(
    blocks, p_ref, raw_ref, taps_ref, shift_ref, sb_ref, rate_ref,
    x_ref, w_ref, bs_ref, dev_ref, keys_ref, queries_ref, gmat_ref, gmat_t_ref,
    step3_ref, cum3_ref, cum_t_ref,
):
    length = blocks * GROUP
    at = pl.program_id(0)
    conv = conv_of(p_ref, taps_ref, shift_ref, length)
    act = conv * sigmoid(conv)

    @pl.when(at == 0)
    def _():
        keys = act[:, :STATE].astype(bf16)
        queries = act[:, STATE:].astype(bf16)
        keys_ref[...] = keys
        queries_ref[...] = queries
        z = raw_ref[...] + sb_ref[0:1, :]
        step = jnp.maximum(z, 0.0) + jnp.log1p(jnp.exp(-jnp.abs(z)))
        decays = -step * rate_ref[0:1, :]
        step3_ref[...] = jnp.concatenate(split3(step), axis=1)
        low = tri(True)
        for b in range(blocks):
            rows = slice(b * GROUP, (b + 1) * GROUP)
            gmat_ref[b] = mm(queries[rows], keys[rows], NT)
            gmat_t_ref[b] = mm(keys[rows], queries[rows], NT)
            parts = split3(decays[rows])
            cum = mm(low, parts[0]) + mm(low, parts[1]) + mm(low, parts[2])
            cum3_ref[rows, :] = jnp.concatenate(split3(cum), axis=1)
            cum_t_ref[:, rows] = sum(
                mm(part, low, ((0,), (1,))) for part in parts
            )

    @pl.when(at > 0)
    def _():
        spread = expander(at - 1)
        step = mm(step3_ref[...], spread)
        cum = mm(cum3_ref[...], spread)
        weighted = act * step
        x_ref[...] = act.astype(bf16)
        w_ref[...] = weighted.astype(bf16)
        ends = mm(spread, lasts(cum3_ref, blocks), ((0,), (1,)))
        total = None
        for b in range(blocks):
            rows = slice(b * GROUP, (b + 1) * GROUP)
            tails = jnp.exp(cum[(b + 1) * GROUP - 1 : (b + 1) * GROUP, :] - cum[rows])
            state = mm((weighted[rows] * tails).astype(bf16), keys_ref[rows, :], TN)
            bs_ref[b] = state
            total = state if total is None else jnp.exp(ends[:, b : b + 1]) * total + state
        dev_ref[...] = total.astype(bf16)


def front(p, raw, taps, shift, sb, rate):
    length = raw.shape[0]
    blocks = length // GROUP
    tile = lambda g: (0, lax.rem(g + TILES, TILES + 1))
    xt = lambda g: (0, jnp.maximum(g - 1, 0))
    whole2 = lambda g: (0, 0)
    whole3 = lambda g: (0, 0, 0)
    return pl.pallas_call(
        functools.partial(front_kernel, blocks),
        grid=(TILES + 1,),
        in_specs=[
            pl.BlockSpec((length + EDGE, TILE), tile),
            pl.BlockSpec((length, HEADS), whole2),
            pl.BlockSpec((CONV, TILE), tile),
            pl.BlockSpec((1, TILE), tile),
            pl.BlockSpec((1, HEADS), whole2),
            pl.BlockSpec((1, HEADS), whole2),
        ],
        out_specs=[
            pl.BlockSpec((length, TILE), xt),
            pl.BlockSpec((length, TILE), xt),
            pl.BlockSpec((blocks, TILE, STATE), lambda g: (0, jnp.maximum(g - 1, 0), 0)),
            pl.BlockSpec((TILE, STATE), lambda g: (jnp.maximum(g - 1, 0), 0)),
            pl.BlockSpec((length, STATE), whole2),
            pl.BlockSpec((length, STATE), whole2),
            pl.BlockSpec((blocks, GROUP, GROUP), whole3),
            pl.BlockSpec((blocks, GROUP, GROUP), whole3),
            pl.BlockSpec((length, 3 * HEADS), whole2),
            pl.BlockSpec((length, 3 * HEADS), whole2),
            pl.BlockSpec((HEADS, length), whole2),
        ],
        out_shape=[
            jax.ShapeDtypeStruct((length, INNER), bf16),
            jax.ShapeDtypeStruct((length, INNER), bf16),
            jax.ShapeDtypeStruct((blocks, INNER, STATE), f32),
            jax.ShapeDtypeStruct((INNER, STATE), bf16),
            jax.ShapeDtypeStruct((length, STATE), bf16),
            jax.ShapeDtypeStruct((length, STATE), bf16),
            jax.ShapeDtypeStruct((blocks, GROUP, GROUP), f32),
            jax.ShapeDtypeStruct((blocks, GROUP, GROUP), f32),
            jax.ShapeDtypeStruct((length, 3 * HEADS), bf16),
            jax.ShapeDtypeStruct((length, 3 * HEADS), bf16),
            jax.ShapeDtypeStruct((HEADS, length), f32),
        ],
        compiler_params=params(),
        cost_estimate=pl.CostEstimate(flops=600_000_000, bytes_accessed=14_000_000, transcendentals=4_000_000),
        name="front",
    )(p, raw, taps, shift, sb, rate)


def intra_kernel(blocks, w_ref, cum3_ref, cum_t_ref, gmat_ref, y_ref):
    at = pl.program_id(0)
    cum = mm(cum3_ref[...], expander(at))
    r = lax.broadcasted_iota(jnp.int32, (GROUP, GROUP), 0)
    c = lax.broadcasted_iota(jnp.int32, (GROUP, GROUP), 1)
    causal = r >= c
    first = lax.broadcasted_iota(jnp.int32, (GROUP, LANES), 1) < HEAD_DIM
    for b in range(blocks):
        rows = slice(b * GROUP, (b + 1) * GROUP)
        gmat = gmat_ref[b]
        for pair in range(HPT // 2):
            lanes = slice(pair * LANES, (pair + 1) * LANES)
            w = w_ref[rows, lanes]
            outs = []
            for side in range(2):
                j = 2 * pair + side
                col = cum[rows, j * HEAD_DIM : j * HEAD_DIM + 1]
                row = cum_t_ref[pl.ds(HPT * at + j, 1), rows]
                kernel = jnp.exp(jnp.where(causal, col - row, -1e30)) * gmat
                outs.append(mm(kernel.astype(bf16), w))
            y_ref[rows, lanes] = jnp.where(first, outs[0], outs[1])


def intra_of(w, cum3, cum_t, gmat):
    length = w.shape[0]
    blocks = length // GROUP
    tile = lambda g: (0, g)
    whole2 = lambda g: (0, 0)
    return pl.pallas_call(
        functools.partial(intra_kernel, blocks),
        grid=(TILES,),
        in_specs=[
            pl.BlockSpec((length, TILE), tile),
            pl.BlockSpec((length, 3 * HEADS), whole2),
            pl.BlockSpec((HEADS, length), whole2),
            pl.BlockSpec((blocks, GROUP, GROUP), lambda g: (0, 0, 0)),
        ],
        out_specs=pl.BlockSpec((length, TILE), tile),
        out_shape=jax.ShapeDtypeStruct((length, INNER), f32),
        compiler_params=params(),
        cost_estimate=pl.CostEstimate(flops=2_200_000_000, bytes_accessed=7_000_000, transcendentals=4_200_000),
        name="intra",
    )(w, cum3, cum_t, gmat)


def middle_kernel(
    blocks, y_ref, x_ref, gate_ref, gno_ref, q_ref, cum3_ref, start_ref, bs_ref, skip_ref, gain_ref,
    no_ref, dgate_ref, do_ref, dgain_ref, dskip_ref, rowsum_ref, dstart_ref, gdev_ref,
    y_s, sq_s, gt_s, r_s, m_s,
):
    length = blocks * GROUP
    phase, at = pl.program_id(0), pl.program_id(1)
    spread = expander(at)
    cum = mm(cum3_ref[...], spread)
    lanes = pl.ds(pl.multiple_of(at * TILE, TILE), TILE)
    x = x_ref[...].astype(f32)
    gate = gate_ref[...]
    sig = sigmoid(gate)
    gn = gno_ref[...]
    gain = gain_ref[0:1, :]
    skip = skip_ref[0:1, :]
    ends = jnp.exp(mm(spread, lasts(cum3_ref, blocks), ((0,), (1,))))

    @pl.when(phase == 0)
    def _():
        start = start_ref[...]
        for b in range(blocks):
            rows = slice(b * GROUP, (b + 1) * GROUP)
            inter = mm(q_ref[rows, :], start.astype(bf16), NT) * jnp.exp(cum[rows])
            y_s[rows, lanes] = y_ref[rows, :] + inter
            start = ends[:, b : b + 1] * start + bs_ref[b]
        gated = (y_s[:, lanes] + skip * x) * (gate * sig)
        sq = gated * gated
        gt = gated * gn * gain
        sq = sq[:, :LANES] + sq[:, LANES:]
        gt = gt[:, :LANES] + gt[:, LANES:]

        @pl.when(at == 0)
        def _():
            sq_s[...] = sq
            gt_s[...] = gt

        @pl.when(at > 0)
        def _():
            sq_s[...] += sq
            gt_s[...] += gt

    @pl.when(phase == 1)
    def _():
        @pl.when(at == 0)
        def _():
            r = lax.rsqrt(jnp.sum(sq_s[...], axis=1, keepdims=True) / INNER + epsilon)
            m = r * r * r * (jnp.sum(gt_s[...], axis=1, keepdims=True) / INNER)
            r_s[...] = jnp.broadcast_to(r, r_s.shape)
            m_s[...] = jnp.broadcast_to(m, m_s.shape)

        r = r_s[:, 0:1]
        m = m_s[:, 0:1]
        y = y_s[:, lanes]
        ssm = y + skip * x
        silu = gate * sig
        gated = ssm * silu
        scaled = gated * r
        no_ref[...] = (scaled * gain).astype(bf16)
        dgain_ref[...] = jnp.sum(gn * scaled, axis=0, keepdims=True)
        dgated = r * gn * gain - gated * m
        dgate_ref[...] = (dgated * ssm * (sig * (1.0 + gate * (1.0 - sig)))).astype(bf16)
        dof = dgated * silu
        dob = dof.astype(bf16)
        do_ref[...] = dob
        dskip_ref[...] = jnp.sum(dof * x, axis=0, keepdims=True)
        sums = head_sums(dob.astype(f32) * y, selector(at))

        @pl.when(at == 0)
        def _():
            rowsum_ref[...] = sums

        @pl.when(at > 0)
        def _():
            rowsum_ref[...] += sums

        scaled_do = (dof * jnp.exp(cum)).astype(bf16)
        total = None
        for b in reversed(range(blocks)):
            rows = slice(b * GROUP, (b + 1) * GROUP)
            d = mm(scaled_do[rows], q_ref[rows, :], TN)
            dstart_ref[b] = d
            total = d if total is None else ends[:, b : b + 1] * total + d
        gdev_ref[...] = total.astype(bf16)


def middle(y, x, gate, gno, q, cum3, start, bs, skip, gain):
    length = x.shape[0]
    blocks = length // GROUP
    both = lambda p, g: (0, g)
    ph0 = lambda p, g: (0, g * (1 - p) + (TILES - 1) * p)
    ph1 = lambda p, g: (0, g * p)
    whole2 = lambda p, g: (0, 0)
    return pl.pallas_call(
        functools.partial(middle_kernel, blocks),
        grid=(2, TILES),
        in_specs=[
            pl.BlockSpec((length, TILE), ph0),
            pl.BlockSpec((length, TILE), both),
            pl.BlockSpec((length, TILE), both),
            pl.BlockSpec((length, TILE), both),
            pl.BlockSpec((length, STATE), whole2),
            pl.BlockSpec((length, 3 * HEADS), whole2),
            pl.BlockSpec((TILE, STATE), lambda p, g: (g * (1 - p) + (TILES - 1) * p, 0)),
            pl.BlockSpec((blocks, TILE, STATE), lambda p, g: (0, g * (1 - p) + (TILES - 1) * p, 0)),
            pl.BlockSpec((1, TILE), both),
            pl.BlockSpec((1, TILE), both),
        ],
        out_specs=[
            pl.BlockSpec((length, TILE), ph1),
            pl.BlockSpec((length, TILE), ph1),
            pl.BlockSpec((length, TILE), ph1),
            pl.BlockSpec((1, TILE), ph1),
            pl.BlockSpec((1, TILE), ph1),
            pl.BlockSpec((length, LANES), whole2),
            pl.BlockSpec((blocks, TILE, STATE), lambda p, g: (0, g * p, 0)),
            pl.BlockSpec((TILE, STATE), lambda p, g: (g * p, 0)),
        ],
        out_shape=[
            jax.ShapeDtypeStruct((length, INNER), bf16),
            jax.ShapeDtypeStruct((length, INNER), bf16),
            jax.ShapeDtypeStruct((length, INNER), bf16),
            jax.ShapeDtypeStruct((1, INNER), f32),
            jax.ShapeDtypeStruct((1, INNER), f32),
            jax.ShapeDtypeStruct((length, LANES), f32),
            jax.ShapeDtypeStruct((blocks, INNER, STATE), f32),
            jax.ShapeDtypeStruct((INNER, STATE), bf16),
        ],
        scratch_shapes=[
            pltpu.VMEM((length, INNER), f32),
            pltpu.VMEM((length, LANES), f32),
            pltpu.VMEM((length, LANES), f32),
            pltpu.VMEM((length, LANES), f32),
            pltpu.VMEM((length, LANES), f32),
        ],
        compiler_params=params(),
        cost_estimate=pl.CostEstimate(flops=1_200_000_000, bytes_accessed=32_000_000, transcendentals=6_000_000),
        name="middle",
    )(y, x, gate, gno, q, cum3, start, bs, skip, gain)


def intra_back_kernel(
    blocks, w_ref, do_ref, cum3_ref, cum_t_ref, gmat_t_ref, k_ref, q_ref, dw_ref, dq_ref, dk_ref, dg_s
):
    at = pl.program_id(0)
    cum = mm(cum3_ref[...], expander(at))
    r = lax.broadcasted_iota(jnp.int32, (GROUP, GROUP), 0)
    c = lax.broadcasted_iota(jnp.int32, (GROUP, GROUP), 1)
    causal = c >= r
    first = lax.broadcasted_iota(jnp.int32, (GROUP, LANES), 1) < HEAD_DIM
    for b in range(blocks):
        rows = slice(b * GROUP, (b + 1) * GROUP)
        gmat = gmat_t_ref[b]
        dg = None
        for pair in range(HPT // 2):
            lanes = slice(pair * LANES, (pair + 1) * LANES)
            w = w_ref[rows, lanes]
            do = do_ref[rows, lanes]
            outs = []
            for side in range(2):
                j = 2 * pair + side
                col = cum[rows, j * HEAD_DIM : j * HEAD_DIM + 1]
                row = cum_t_ref[pl.ds(HPT * at + j, 1), rows]
                decay = jnp.exp(jnp.where(causal, row - col, -1e30))
                outs.append(mm((decay * gmat).astype(bf16), do))
                own = jnp.where(first if side == 0 else ~first, w, jnp.zeros_like(w))
                term = mm(own, do, NT) * decay
                dg = term if dg is None else dg + term
            dw_ref[rows, lanes] = jnp.where(first, outs[0], outs[1])

        @pl.when(at == 0)
        def _():
            dg_s[b] = dg

        @pl.when(at > 0)
        def _():
            dg_s[b] += dg

    @pl.when(at == TILES - 1)
    def _():
        for b in range(blocks):
            rows = slice(b * GROUP, (b + 1) * GROUP)
            dg = dg_s[b].astype(bf16)
            dk_ref[rows, :] = mm(dg, q_ref[rows, :])
            dq_ref[rows, :] = mm(dg, k_ref[rows, :], TN)


def intra_back(w, do, cum3, cum_t, gmat_t, k, q):
    length = w.shape[0]
    blocks = length // GROUP
    tile = lambda g: (0, g)
    whole2 = lambda g: (0, 0)
    return pl.pallas_call(
        functools.partial(intra_back_kernel, blocks),
        grid=(TILES,),
        in_specs=[
            pl.BlockSpec((length, TILE), tile),
            pl.BlockSpec((length, TILE), tile),
            pl.BlockSpec((length, 3 * HEADS), whole2),
            pl.BlockSpec((HEADS, length), whole2),
            pl.BlockSpec((blocks, GROUP, GROUP), lambda g: (0, 0, 0)),
            pl.BlockSpec((length, STATE), whole2),
            pl.BlockSpec((length, STATE), whole2),
        ],
        out_specs=[
            pl.BlockSpec((length, TILE), tile),
            pl.BlockSpec((length, STATE), whole2),
            pl.BlockSpec((length, STATE), whole2),
        ],
        out_shape=[
            jax.ShapeDtypeStruct((length, INNER), f32),
            jax.ShapeDtypeStruct((length, STATE), f32),
            jax.ShapeDtypeStruct((length, STATE), f32),
        ],
        scratch_shapes=[pltpu.VMEM((blocks, GROUP, GROUP), f32)],
        compiler_params=params(),
        cost_estimate=pl.CostEstimate(flops=4_400_000_000, bytes_accessed=10_000_000, transcendentals=4_200_000),
        name="intra_back",
    )(w, do, cum3, cum_t, gmat_t, k, q)


def back_kernel(
    blocks, p_ref, taps_ref, shift_ref, x_ref, w_ref, do_ref, dwi_ref, skip_ref,
    start_ref, bs_ref, adj_ref, dstart_ref,
    k_ref, q_ref, step3_ref, cum3_ref, dqi_ref, dki_ref, rowsum_ref, raw_ref, sb_ref, rate_ref,
    gp_ref, last_ref, before_ref, dtaps_ref, dshift_ref, draw_ref, dsb_ref, drate_ref,
    dq_s, dk_s, sx_s, sw_s, sv_s, dec_s, d_s,
):
    length = blocks * GROUP
    at = pl.program_id(0)

    @pl.when(at == 0)
    def _():
        dq_s[...] = dqi_ref[...]
        dk_s[...] = dki_ref[...]
        sx_s[...] = jnp.zeros_like(sx_s)
        sw_s[...] = jnp.zeros_like(sw_s)
        sv_s[...] = jnp.zeros_like(sv_s)
        dec_s[...] = jnp.zeros_like(dec_s)
        d_s[0:EDGE, :] = jnp.zeros((EDGE, TILE), f32)
        d_s[length + EDGE :, :] = jnp.zeros((EDGE, TILE), f32)

    def conv_back(dact):
        conv = conv_of(p_ref, taps_ref, shift_ref, length)
        sig = sigmoid(conv)
        dconv = dact * (sig * (1.0 + conv * (1.0 - sig)))
        d_s[EDGE : EDGE + length, :] = dconv
        dshift_ref[...] = jnp.sum(dconv, axis=0, keepdims=True)
        dp = None
        before = None
        for k in range(CONV):
            tap = taps_ref[k : k + 1, :]
            src = p_ref[pl.ds(EDGE - CONV + 1 + k, length), :]
            dtaps_ref[k : k + 1, :] = jnp.sum(dconv * src, axis=0, keepdims=True)
            term = tap * d_s[pl.ds(EDGE + CONV - 1 - k, length), :]
            dp = term if dp is None else dp + term
            edge = tap * d_s[pl.ds(CONV - 1 - k, EDGE), :]
            before = edge if before is None else before + edge
        gp_ref[...] = dp.astype(bf16)
        last_ref[...] = dp[length - EDGE :, :]
        before_ref[...] = before

    @pl.when(at < TILES)
    def _():
        spread = expander(at)
        sel = selector(at)
        cum = mm(cum3_ref[...], spread)
        step = mm(step3_ref[...], spread)
        ends = jnp.exp(mm(spread, lasts(cum3_ref, blocks), ((0,), (1,))))
        x = x_ref[...].astype(f32)
        w = w_ref[...].astype(f32)
        do = do_ref[...].astype(f32)
        scaled_do = (do * jnp.exp(cum)).astype(bf16)
        starts = [start_ref[...]]
        for b in range(blocks - 1):
            starts.append(ends[:, b : b + 1] * starts[b] + bs_ref[b])
        adjs = [None] * blocks
        adj = adj_ref[...]
        for b in reversed(range(blocks)):
            adjs[b] = adj
            adj = ends[:, b : b + 1] * adj + dstart_ref[b]
        dws = []
        for b in range(blocks):
            rows = slice(b * GROUP, (b + 1) * GROUP)
            tails = jnp.exp(cum[(b + 1) * GROUP - 1 : (b + 1) * GROUP, :] - cum[rows])
            ab = adjs[b].astype(bf16)
            dws.append(tails * mm(k_ref[rows, :], ab, NT))
            dk_s[rows, :] += mm((w[rows] * tails).astype(bf16), ab)
            dq_s[rows, :] += mm(scaled_do[rows], starts[b].astype(bf16))
            hi, lo = split2(ends[:, b : b + 1] * adjs[b] * starts[b])
            dec_s[b : b + 1, :] += jnp.sum(mm(hi, sel, TN) + mm(lo, sel, TN), axis=0, keepdims=True)
        dws = jnp.concatenate(dws, axis=0)
        dw = dwi_ref[...] + dws
        sx_s[...] += head_sums(dw * x, sel)
        sw_s[...] += head_sums(dw * w, sel)
        sv_s[...] += head_sums(dws * w, sel)
        conv_back(dw * step + do * skip_ref[0:1, :])

    @pl.when(at == TILES)
    def _():
        conv_back(jnp.concatenate([dk_s[...], dq_s[...]], axis=1))
        dcum = (rowsum_ref[...] - sw_s[...])[:, :HEADS]
        sv = sv_s[...][:, :HEADS]
        z = raw_ref[...] + sb_ref[0:1, :]
        step = jnp.maximum(z, 0.0) + jnp.log1p(jnp.exp(-jnp.abs(z)))
        rate = rate_ref[0:1, :]
        up = tri(False)
        decays = []
        for b in range(blocks):
            rows = slice(b * GROUP, (b + 1) * GROUP)
            parts = split3(dcum[rows])
            extra = jnp.sum(sv[rows], axis=0, keepdims=True) + dec_s[b : b + 1, :HEADS]
            decays.append(mm(up, parts[0]) + mm(up, parts[1]) + mm(up, parts[2]) + extra)
        ddecay = jnp.concatenate(decays, axis=0)
        dstep = sx_s[...][:, :HEADS] - ddecay * rate
        dz = dstep * sigmoid(z)
        draw_ref[...] = dz.astype(bf16)
        dsb_ref[...] = jnp.sum(dz, axis=0, keepdims=True)
        drate_ref[...] = jnp.sum(-ddecay * step * rate, axis=0, keepdims=True)


def back(p, taps, shift, x, w, do, dwi, skip, start, bs, adj, dstart, k, q, step3, cum3, dqi, dki, rowsum, raw, sb, rate):
    length = x.shape[0]
    blocks = length // GROUP
    tile = lambda g: (0, g)
    xt = lambda g: (0, jnp.minimum(g, TILES - 1))
    st = lambda g: (jnp.minimum(g, TILES - 1), 0)
    st3 = lambda g: (0, jnp.minimum(g, TILES - 1), 0)
    whole2 = lambda g: (0, 0)
    spec = pl.BlockSpec
    return pl.pallas_call(
        functools.partial(back_kernel, blocks),
        grid=(TILES + 1,),
        in_specs=[
            spec((length + EDGE, TILE), tile),
            spec((CONV, TILE), tile),
            spec((1, TILE), tile),
            spec((length, TILE), xt),
            spec((length, TILE), xt),
            spec((length, TILE), xt),
            spec((length, TILE), xt),
            spec((1, TILE), xt),
            spec((TILE, STATE), st),
            spec((blocks, TILE, STATE), st3),
            spec((TILE, STATE), st),
            spec((blocks, TILE, STATE), st3),
            spec((length, STATE), whole2),
            spec((length, STATE), whole2),
            spec((length, 3 * HEADS), whole2),
            spec((length, 3 * HEADS), whole2),
            spec((length, STATE), whole2),
            spec((length, STATE), whole2),
            spec((length, LANES), whole2),
            spec((length, HEADS), whole2),
            spec((1, HEADS), whole2),
            spec((1, HEADS), whole2),
        ],
        out_specs=[
            spec((length, TILE), tile),
            spec((EDGE, TILE), tile),
            spec((EDGE, TILE), tile),
            spec((CONV, TILE), tile),
            spec((1, TILE), tile),
            spec((length, HEADS), whole2),
            spec((1, HEADS), whole2),
            spec((1, HEADS), whole2),
        ],
        out_shape=[
            jax.ShapeDtypeStruct((length, CONV_CH), bf16),
            jax.ShapeDtypeStruct((EDGE, CONV_CH), f32),
            jax.ShapeDtypeStruct((EDGE, CONV_CH), f32),
            jax.ShapeDtypeStruct((CONV, CONV_CH), f32),
            jax.ShapeDtypeStruct((1, CONV_CH), f32),
            jax.ShapeDtypeStruct((length, HEADS), bf16),
            jax.ShapeDtypeStruct((1, HEADS), f32),
            jax.ShapeDtypeStruct((1, HEADS), f32),
        ],
        scratch_shapes=[
            pltpu.VMEM((length, STATE), f32),
            pltpu.VMEM((length, STATE), f32),
            pltpu.VMEM((length, LANES), f32),
            pltpu.VMEM((length, LANES), f32),
            pltpu.VMEM((length, LANES), f32),
            pltpu.VMEM((8, LANES), f32),
            pltpu.VMEM((length + 2 * EDGE, TILE), f32),
        ],
        compiler_params=params(),
        cost_estimate=pl.CostEstimate(flops=2_500_000_000, bytes_accessed=32_000_000, transcendentals=6_000_000),
        name="back",
    )(p, taps, shift, x, w, do, dwi, skip, start, bs, adj, dstart, k, q, step3, cum3, dqi, dki, rowsum, raw, sb, rate)


def carried(decay, state, axis, reverse):
    size, here = lax.axis_size(axis), lax.axis_index(axis)
    rows = lambda d: jnp.repeat(d, HEAD_DIM)[:, None]
    if size == 4:
        core, x = here % 2, here // 2
        swap = [(i, i ^ 1) for i in range(4)]
        mate, mate_decay = lax.ppermute(state, axis, swap), lax.ppermute(decay, axis, swap)
        own, other = state.astype(f32), mate.astype(f32)
        ahead = (core == 0) if reverse else (core == 1)
        pair = jnp.where(
            ahead,
            rows(decay) * other + own,
            rows(mate_decay) * own + other,
        ).astype(bf16)
        route = [(2, 0), (3, 1)] if reverse else [(0, 2), (1, 3)]
        far = lax.ppermute(pair, axis, route).astype(f32)
        near = jnp.where(ahead, other, 0.0)
        return near + jnp.where(ahead, rows(mate_decay), 1.0) * far
    states = lax.all_gather(state, axis)
    decays = lax.all_gather(decay, axis)

    def one(lap, total):
        at = size - 1 - lap if reverse else lap
        use = at > here if reverse else at < here
        new = rows(decays[at]) * total + states[at].astype(f32)
        return jnp.where(use, new, total)

    return lax.fori_loop(0, size, one, jnp.zeros(state.shape, f32))


def rms_scale(values, gains):
    return values * lax.rsqrt(jnp.mean(values * values, axis=-1, keepdims=True) + epsilon) * gains


def gather_rows(shard):
    return lax.all_gather(shard, "dp", axis=0, tiled=True)


def reduce_rows(full):
    part = lax.psum_scatter(full.astype(bf16), "dp", scatter_dimension=0, tiled=True)
    return lax.psum(part, "seq").astype(f32)


def shards(
    tokens, cotangent, in_weight, out_weight, conv_weight, conv_bias,
    pre_gain, norm_gain, step_bias, decay_log, skip_gain,
):
    dp = lax.axis_size("dp")
    seq = lax.axis_size("seq")
    width = tokens.shape[2]
    pieces = [
        conv_weight, conv_bias, pre_gain, norm_gain, step_bias, decay_log, skip_gain,
        in_weight[:, INNER + CONV_CH :],
    ]
    shapes = [piece.shape for piece in pieces]
    sizes = [piece.size for piece in pieces]
    used = sum(sizes)
    padded = -(-used // 2048) * 2048
    flat = jnp.concatenate([piece.reshape(-1) for piece in pieces] + [jnp.zeros((padded - used,), bf16)])
    small = lax.all_gather(flat, "dp")
    got, at = [], 0
    for shape, size in zip(shapes, sizes):
        got.append(small[:, at : at + size].reshape((dp,) + shape))
        at += size
    taps = jnp.moveaxis(got[0], 0, 1).reshape(CONV, CONV_CH).astype(f32)
    shift, gains_pre, gains_norm, bias_step, log_rates, skip = [
        piece.reshape(-1).astype(f32) for piece in got[1:7]
    ]
    step_weight = got[7].reshape(width, HEADS)
    conv_full = gather_rows(in_weight[:, INNER : INNER + CONV_CH])
    gate_full = gather_rows(in_weight[:, :INNER])
    out_full = gather_rows(out_weight)
    shift = shift[None]
    rate = jnp.exp(log_rates)[None]
    bias_step = bias_step[None]
    skip_lanes = jnp.repeat(skip, HEAD_DIM)[None]

    toks = tokens[0]
    length = toks.shape[0]
    edge = lax.ppermute(toks[length - EDGE :], "seq", [(i, i + 1) for i in range(seq - 1)])
    normed_ext = rms_scale(jnp.concatenate([edge, toks], axis=0).astype(f32), gains_pre).astype(bf16)
    normed = normed_ext[EDGE:]
    p = jnp.dot(normed_ext, conv_full, preferred_element_type=f32)
    raw = jnp.dot(normed, step_weight, preferred_element_type=f32)
    x, w, bs, dev, k, q, gmat, gmat_t, step3, cum3, cum_t = front(p, raw, taps, shift, bias_step, rate)
    blocks = length // GROUP
    dev_decay = jnp.exp(sum(cum_t[:, (b + 1) * GROUP - 1] for b in range(blocks)))
    start = carried(dev_decay, dev, "seq", False)
    y = intra_of(w, cum3, cum_t, gmat)
    gate = jnp.dot(normed, gate_full, preferred_element_type=f32)
    cot = cotangent[0]
    gno = lax.dot_general(cot, out_full, (((1,), (1,)), ((), ())), preferred_element_type=f32)
    no, dgate, do, dgain, dskip, rowsum, dstart, gdev = middle(
        y, x, gate, gno, q, cum3, start, bs, skip_lanes, gains_norm[None]
    )
    adj = carried(dev_decay, gdev, "seq", True)
    rows = toks.astype(f32)
    mixed = (rows + jnp.dot(no, out_full, preferred_element_type=f32)).astype(bf16)
    over_rows = (((0,), (0,)), ((), ()))
    grad_out = reduce_rows(lax.dot_general(no, cot, over_rows, preferred_element_type=f32))
    grad_gate = reduce_rows(lax.dot_general(normed, dgate, over_rows, preferred_element_type=f32))
    dwi, dqi, dki = intra_back(w, do, cum3, cum_t, gmat_t, k, q)
    gp, last, before, dtaps, dshift, draw, dsb, drate = back(
        p, taps, shift, x, w, do, dwi, skip_lanes, start, bs, adj, dstart,
        k, q, step3, cum3, dqi, dki, rowsum, raw, bias_step, rate,
    )
    returned = lax.ppermute(before, "seq", [(i + 1, i) for i in range(seq - 1)])
    gp = gp.at[length - EDGE :].set((last + returned).astype(bf16))
    grad_conv = reduce_rows(lax.dot_general(normed, gp, over_rows, preferred_element_type=f32))
    grad_step = lax.dot_general(normed, draw, over_rows, preferred_element_type=f32)
    over_cols = (((1,), (1,)), ((), ()))
    dnormed = (
        lax.dot_general(gp, conv_full, over_cols, preferred_element_type=f32)
        + lax.dot_general(dgate, gate_full, over_cols, preferred_element_type=f32)
        + lax.dot_general(draw, step_weight, over_cols, preferred_element_type=f32)
    )
    r = lax.rsqrt(jnp.mean(rows * rows, axis=-1, keepdims=True) + epsilon)
    t = dnormed * gains_pre
    drows = r * t - rows * (r * r * r * jnp.mean(rows * t, axis=-1, keepdims=True))
    grad_tokens = (cot.astype(f32) + drows).astype(bf16)
    dpre = jnp.sum(dnormed * rows * r, axis=0)

    smalls = [
        jnp.moveaxis(dtaps.reshape(CONV, dp, -1), 1, 0).reshape(dp, -1),
        dshift.reshape(dp, -1),
        dpre.reshape(dp, -1),
        dgain.reshape(dp, -1),
        dsb.reshape(dp, -1),
        drate.reshape(dp, -1),
        jnp.sum(dskip.reshape(HEADS, HEAD_DIM), axis=1).reshape(dp, -1),
        grad_step.reshape(dp, -1),
    ]
    bundle = jnp.concatenate(smalls + [jnp.zeros((dp, padded - used), f32)], axis=1).astype(bf16)
    mine = lax.psum(lax.psum_scatter(bundle, "dp", scatter_dimension=0), "seq").astype(f32)
    outs, at = [], 0
    for shape, size in zip(shapes, sizes):
        outs.append(mine[at : at + size].reshape(shape))
        at += size
    grad_in = jnp.concatenate([grad_gate, grad_conv, outs[7]], axis=1)
    return (
        mixed[None], grad_tokens[None], grad_in, grad_out, outs[0], outs[1],
        outs[2], outs[3], outs[4], outs[5], outs[6],
    )


def solution(mesh):
    return jax.shard_map(
        shards,
        mesh=mesh,
        in_specs=(
            P("dp", "seq", None), P("dp", "seq", None), P("dp", None), P("dp", None),
            P(None, "dp"), P("dp"), P("dp"), P("dp"), P("dp"), P("dp"), P("dp"),
        ),
        out_specs=(
            P("dp", "seq", None), P("dp", "seq", None), P("dp", None), P("dp", None),
            P(None, "dp"), P("dp"), P("dp"), P("dp"), P("dp"), P("dp"), P("dp"),
        ),
        check_vma=False,
    )
```

time: 895 us -> 713 us (0.80)
  blocking collectives: 150 us -> 42.8 us
  other arithmetic: 112 us -> 15.1 us
  matrix products: 153 us -> 57.3 us
  waiting for transfers between devices: 355 us -> 442 us
  Pallas kernels: 0 us -> 81.4 us
  local copies, waits for them, and re-layouts: 90.7 us -> 41.6 us
    dot_general x18 -> x12, matrix products: 153 us -> 57.3 us  [the longest x1 7.09 us: shards(): lax.dot_general(cot, out_full, (((1,), (1,)), ((), ())), preferred_elemen...]
    reduce_scatter x1 -> x3, waiting for transfers between devices: 88.6 us -> 177 us  [reduce_rows(): lax.psum_scatter(full.astype(bf16), 'dp', scatter_dimension=0, tiled=True)]
    unnamed x10 -> x9, waiting for transfers between devices: 157 us -> 70.8 us
    all_gather x4 -> x3, waiting for transfers between devices: 73.1 us -> 159 us  [gather_rows(): return lax.all_gather(shard, 'dp', axis=0, tiled=True)]
    pallas_call x0 -> x5, Pallas kernels: none -> 81.4 us  [the longest x1 27.7 us: back(): pl.pallas_call(functools.partial(back_kernel, blocks), grid=(TILES + 1,),...]
    unnamed x3 -> x0, blocking collectives: 60.2 us -> none
    all_gather x3 -> x1, blocking collectives: 83.8 us -> 32.2 us  [shards(): small = lax.all_gather(flat, 'dp')]
    reduce_sum x9 -> x2, other arithmetic: 43.4 us -> 0.4 us  [the longest x1 0.28 us: shards(): r = lax.rsqrt(jnp.mean(rows * rows, axis=-1, keepdims=True) + epsilon)]
  transfers between devices with their start and end apart: 10 -> 15, of which waited for: 6 -> 10; matrix products, arithmetic and copies ran while one was open for 15% -> 11% of each run, Pallas kernels for 0% -> 8%
where the time goes in v1:
time: 713 us; the launch traced here: 706 us
  waiting for transfers between devices  442 us (62%)
  Pallas kernels  81.4 us (11%)
  matrix products  57.3 us (8%)
  blocking collectives  42.8 us (6%)
  local copies, waits for them, and re-layouts  41.6 us (6%)
  between operations  15.4 us (2%)
  other arithmetic  15.1 us (2%)
  starting transfers between devices  9.57 us (1%)
    reduce_scatter x3, waiting for transfers between devices, reduce_rows(): lax.psum_scatter(full.astype(bf16), 'dp', scatter_dimension=0, tiled=True)  177 us
    all_gather x3, waiting for transfers between devices, gather_rows(): return lax.all_gather(shard, 'dp', axis=0, tiled=True)  159 us
    unnamed x9, waiting for transfers between devices  70.8 us
    all_gather x1, blocking collectives, shards(): small = lax.all_gather(flat, 'dp')  32.2 us
    psum x1, waiting for transfers between devices, reduce_rows(): return lax.psum(part, 'seq').astype(f32)  30.6 us
    pallas_call x1, Pallas kernels, back(): pl.pallas_call(functools.partial(back_kernel, blocks), grid=(TILES + 1,),...  27.7 us
    unnamed x135, local copies, waits for them, and re-layouts  25.3 us
    pallas_call x1, Pallas kernels, middle(): pl.pallas_call(functools.partial(middle_kernel, blocks), grid=(2, TILES),...  23 us
  transfers between devices with their start and end apart: 15, of which 10 were waited for; matrix products, arithmetic and copies ran while one was open for 11% of the time, Pallas kernels for 8%

profile of v1, /device:TPU:0, one launch (start us, length us, event | category | flops | bytes accessed | tf_op | source)
XLA Modules:
  0.0 705.5 jit_solution(16647529264737054713)
XLA Ops:
  7.3 2.1 slice.93
  9.5 0.8 slice.100
  11.1 2.4 collective-permute-start
  14.0 32.2 %all-gather = bf16[49152]{0:T(1024)(128)(2,1)S(1)} all-gather(bf16[6144]{0:T(1024)(128)(2,1)S(1)} %concatenate.16), channel_id=2, replica_groups=mesh['dp'=8,'seq'=4] {'dp'}, dimensions={0}, use_global_device_ids=true | all-gather | bytes 110592 | tf_op jit(solution)/shard_map/all_gather | solution.py:691
  48.7 46.8 %all-gather.5.cloned.1.call-done = bf16[1024,2304]{0,1:T(8,128)(2,1)} async-done(((bf16[128,2304]{0,1:T(8,128)(2,1)}), bf16[1024,2304]{0,1:T(8,128)(2,1)}) %all-gather.5.cloned.1.call-update) | async-done | bytes 4718608 | tf_op jit(solution)/shard_map/all_gather | solution.py:667
  95.5 5.1 fusion.33.p_ref
  100.6 13.3 %front.1 = (bf16[512,2048]{1,0:T(8,128)(2,1)S(1)}, bf16[512,2048]{1,0:T(8,128)(2,1)S(1)}, f32[2,2048,128]{2,1,0:T(8,128)S(1)}, bf16[2048,128]{1,0:T(8,128)(2,1)S...) custom-call(f32[528,2304]{1,0:T(8,128)S(1)} %fusion.33.p_ref, ...), custom_call_target="tpu_custom_call" | custom-call | flops 600000000 | bytes 14000000 | tf_op jit(solution)/shard_map/front/pallas_call | solution.py:152
  113.9 1.3 copy-done
  115.2 1.3 copy-done.5
  116.5 0.8 copy-done.32
  117.3 0.8 copy-done.34
  118.1 53.2 %all-gather.7.cloned.1.call-done = bf16[1024,2048]{0,1:T(8,128)(2,1)} async-done(((bf16[128,2048]{0,1:T(8,128)(2,1)}), bf16[1024,2048]{0,1:T(8,128)(2,1)}) %all-gather.7.cloned.1.call-update) | async-done | bytes 4194320 | tf_op jit(solution)/shard_map/all_gather | solution.py:667
  171.4 6.9 fusion.25.gate_ref
  178.7 1.0 collective-permute-done.2
  179.8 2.4 fusion.13
  182.2 3.7 collective-permute-start.3
  185.9 59.2 %all-gather.9.cloned.1.call-done = bf16[2048,1024]{1,0:T(8,128)(2,1)} async-done(((bf16[256,1024]{1,0:T(8,128)(2,1)}), bf16[2048,1024]{1,0:T(8,128)(2,1)}) %all-gather.9.cloned.1.call-update) | async-done | bytes 4194320 | tf_op jit(solution)/shard_map/all_gather | solution.py:667
  245.1 7.1 %fusion.20.gno_ref = f32[512,2048]{1,0:T(8,128)} fusion(bf16[2048,1024]{1,0:T(8,128)(2,1)} %all-gather.9.cloned.1.call-done, bf16[1,512,1024]{2,1,0:T(8,128)(2,1)} %param.14), kind=kOutput, calls=%fused_computation.44 | convolution fusion | flops 2147483648 | bytes 9437184 | tf_op jit(solution)/shard_map/dot_general | solution.py:723
  252.2 6.5 intra.1.y_ref
  258.7 2.0 copy-done.4
  261.3 0.8 copy-done.48
  262.1 1.5 fusion.16.start_ref
  263.7 23.0 %middle.1 = (bf16[512,2048]{1,0:T(8,128)(2,1)S(1)}, bf16[512,2048]{1,0:T(8,128)(2,1)S(1)}, bf16[512,2048]{1,0:T(8,128)(2,1)S(1)}, f32[1,2048]{1,0:T(1,128)S(1)},...) custom-call(f32[512,2048]{1,0:T(8,128)} %copy-done.4, ...), custom_call_target="tpu_custom_call" | custom-call | flops 1200000000 | bytes 32000000 | tf_op jit(solution)/shard_map/middle/pallas_call | solution.py:333
  286.7 1.3 copy-done.9
  288.0 1.3 copy-done.11
  289.3 0.8 copy-done.12
  290.1 0.7 copy-done.15
  290.8 1.3 copy-done.28
  292.1 1.4 copy-done.30
  293.5 4.4 convolution_convert_fusion.2
  298.0 6.3 convolution_convert_fusion.1
  304.4 2.1 collective-permute-done.4
  306.5 1.7 fusion.15
  308.2 1.5 collective-permute-start.5
  309.7 1.6 copy-done.7
  311.3 1.6 copy-done.10
  312.9 0.9 copy-done.18
  313.8 1.0 copy-done.35
  314.9 10.9 %intra_back.1 = (f32[512,2048]{1,0:T(8,128)S(1)}, f32[512,128]{1,0:T(8,128)S(1)}, f32[512,128]{1,0:T(8,128)S(1)}) custom-call(bf16[512,2048]{1,0:T(8,128)(2,1)S(1)} %copy-done.7, bf16[512,2048]{1,0:T(8,128)(2,1)S(1)} %copy-done.10, bf16[512,96]{1,0:T(8,128)(2,1)S(1)} %get-tuple-element.54.cum3_ref, f32[32,512]{1,0:T(8,128)S(1)} %get-tuple-element.55.cum_t_ref, ...), custom_call_target="tpu_custom_call" | custom-call | flops 4400000000 | bytes 10000000 | tf_op jit(solution)/shard_map/intra_back/pallas_call | solution.py:432
  325.8 2.1 copy-done.3
  328.3 1.2 copy-done.1
  329.5 27.7 %back.1 = (bf16[512,2304]{1,0:T(8,128)(2,1)}, f32[16,2304]{1,0:T(8,128)S(1)}, f32[16,2304]{1,0:T(8,128)S(1)}, f32[4,2304]{1,0:T(4,128)S(1)}, f32[1,2304]{1,0:T(1...) custom-call(f32[528,2304]{1,0:T(8,128)} %copy-done.2, ...), custom_call_target="tpu_custom_call" | custom-call | flops 2500000000 | bytes 32000000 | tf_op jit(solution)/shard_map/back/pallas_call | solution.py:570
  357.2 1.3 collective-permute-start.6
  358.5 2.0 collective-permute-done.6
  361.1 6.0 convolution_convert_fusion
  370.1 0.7 reshape.228
  371.4 5.9 fusion.35
  378.7 1.6 convolution_convert_fusion.3
  380.4 0.9 reshape.229
  381.5 0.7 reshape.221
  382.3 5.4 fusion.34
  387.8 2.8 fusion.10
  390.5 1.7 concatenate.17
  392.3 5.5 fusion.11
  397.8 78.2 %reduce-scatter.8.cloned.1.call-done = bf16[256,1024]{1,0:T(8,128)(2,1)} async-done(((bf16[2048,1024]{1,0:T(8,128)(2,1)}), bf16[256,1024]{1,0:T(8,128)(2,1)}) %reduce-scatter.8.cloned.1.call-update) | async-done | bytes 524304 | tf_op jit(solution)/shard_map/reduce_scatter | solution.py:671
  476.0 98.5 %reduce-scatter.6.cloned.1.call-done = bf16[128,2304]{1,0:T(8,128)(2,1)} async-done(((bf16[1024,2304]{1,0:T(8,128)(2,1)}), bf16[128,2304]{1,0:T(8,128)(2,1)}) %reduce-scatter.6.cloned.1.call-update) | async-done | bytes 589840 | tf_op jit(solution)/shard_map/reduce_scatter | solution.py:671
  574.6 3.1 fusion.18
  577.8 70.0 %all-reduce.5.cloned.1.call-done = bf16[8,6144]{1,0:T(8,128)(2,1)} async-done(((bf16[8,6144]{1,0:T(8,128)(2,1)}), bf16[8,6144]{1,0:T(8,128)(2,1)}) %all-reduce.5.cloned.1.call-update) | async-done | bytes 98320
  647.7 1.6 dynamic-slice_reduce_fusion
  649.4 10.6 %psum.30 = bf16[6144]{0:T(1024)(128)(2,1)S(1)} all-reduce(bf16[6144]{0:T(1024)(128)(2,1)S(1)} %dynamic-slice_reduce_fusion), channel_id=1, replica_groups=mesh['dp'=8,'seq'=4] {'seq'}, use_global_device_ids=true, to_apply=%region_10.11 | all-reduce | flops 6144 | bytes 24576 | tf_op jit(solution)/shard_map/psum | solution.py:765
  663.2 30.6 %all-reduce.7.cloned.1.call-done = (bf16[128,2304]{1,0:T(8,128)(2,1)}, bf16[128,2048]{1,0:T(8,128)(2,1)}, bf16[256,1024]{1,0:T(8,128)(2,1)}) async-done(((bf16[128,2304]{1,0:T(8,128)(2,1)}, bf16[128,2048]{1,0:T(8,128)(2,1)}, bf16[256,1024]{1,0:T(8,128)(2,1)}), (bf16[128,2304]{1,0:T(8,128)(2,1)}, bf16[128,2048]{1,0:T(8,128)(2,1)}, bf16[256,1024]{1,0:T(8,128)(2,1)})) %all-reduce.7.cloned.1.call-update) | async-done | bytes 1638416 | tf_op jit(solution)/shard_map/psum | solution.py:672
  693.7 1.2 convert_element_type.175
  695.2 2.0 copy.39
  697.2 1.1 convert_element_type.178
  (207 shorter events, 15.0 us)
Async XLA Ops:
  7.2 2.3 copy-start.39
  7.2 6.3 slice-start
  7.2 3.9 copy-start.36
  7.2 6.5 copy-start.58
  7.2 6.6 copy-start.59
  7.2 6.6 copy-start.60
  7.2 6.6 copy-start.61
  7.3 6.6 copy-start.62
  7.3 6.6 copy-start.63
  7.3 6.6 copy-start.64
  7.3 88.2 %all-gather.5.cloned.1.call-start = ((), (), s32[]{:S(2)}) async-start(), calls=%async_computation.3 | async-start | bytes 5308416 | tf_op jit(solution)/shard_map/all_gather | solution.py:667
  9.4 161.9 %all-gather.7.cloned.1.call-start = ((), (), s32[]{:S(2)}) async-start(), calls=%async_computation.4 | async-start | bytes 4718592 | tf_op jit(solution)/shard_map/all_gather | solution.py:667
  10.3 234.8 %all-gather.9.cloned.1.call-start = ((), (), s32[]{:S(2)}) async-start(), calls=%async_computation.5 | async-start | bytes 4718592 | tf_op jit(solution)/shard_map/all_gather | solution.py:667
  11.1 386.7 %reduce-scatter.4.cloned.1.call-start = ((), (), s32[]{:S(2)}) async-start(), calls=%async_computation.6 | async-start | bytes 4718592 | tf_op jit(solution)/shard_map/reduce_scatter | solution.py:671
  11.1 36.4 %collective-permute-start = (bf16[16,1024]{1,0:T(8,128)(2,1)S(1)}, bf16[16,1024]{1,0:T(8,128)(2,1)S(1)}, u32[]{:S(2)}, u32[]{:S(2)}) collective-permute-start(bf16[16,1024]{1,0:T(8,128)(2,1)S(1)} %slice_bitcast_fusion), channel_id=1, source_target_pairs={{0,1},{1,2},{2,3},{4,5},{5,6},{6,7},{8,9},{9,10},{10,11},{12,13},{... | collective-permute-start | bytes 98312 | tf_op jit(solution)/shard_map/ppermute | solution.py:711
  46.3 1.9 copy-start.52
  46.8 1.8 copy-start.44
  46.9 53.7 %copy-start.24 = (f32[1,32]{1,0:T(1,128)}, f32[1,32]{1,0:T(1,128)S(1)}, u32[]{:S(2)}) copy-start(f32[1,32]{1,0:T(1,128)S(1)} %reshape.235.sb_ref) | copy-start | bytes 388
  47.3 53.3 %copy-start.26 = (f32[1,32]{1,0:T(1,128)}, f32[1,32]{1,0:T(1,128)S(1)}, u32[]{:S(2)}) copy-start(f32[1,32]{1,0:T(1,128)S(1)} %exp.20.rate_ref) | copy-start | bytes 388
  48.2 47.3 %copy-start.40 = (bf16[528,1024]{1,0:T(8,128)(2,1)}, bf16[528,1024]{1,0:T(8,128)(2,1)S(1)}, u32[]{:S(2)}) copy-start(bf16[528,1024]{1,0:T(8,128)(2,1)S(1)} %fusion.2) | copy-start | bytes 3244036
  48.7 51.9 %copy-start.13 = (f32[512,32]{1,0:T(8,128)}, f32[512,32]{1,0:T(8,128)S(1)}, u32[]{:S(2)}) copy-start(f32[512,32]{1,0:T(8,128)S(1)} %fusion.27.raw_ref) | copy-start | bytes 196612
  100.6 13.3 %copy-start.2 = (f32[528,2304]{1,0:T(8,128)}, f32[528,2304]{1,0:T(8,128)S(1)}, u32[]{:S(2)}) copy-start(f32[528,2304]{1,0:T(8,128)S(1)} %fusion.33.p_ref) | copy-start | bytes 14598148
  118.1 60.1 %copy-start.17 = (bf16[512,128]{1,0:T(8,128)(2,1)}, bf16[512,128]{1,0:T(8,128)(2,1)S(1)}, u32[]{:S(2)}) copy-start(bf16[512,128]{1,0:T(8,128)(2,1)S(1)} %get-tuple-element.64.k_ref) | copy-start | bytes 393220
  118.1 60.1 %copy-start.20 = (bf16[512,96]{1,0:T(8,128)(2,1)}, bf16[512,96]{1,0:T(8,128)(2,1)S(1)}, u32[]{:S(2)}) copy-start(bf16[512,96]{1,0:T(8,128)(2,1)S(1)} %get-tuple-element.68.step3_ref) | copy-start | bytes 294916
  118.1 61.7 %collective-permute-start.1 = (bf16[2048,128]{1,0:T(8,128)(2,1)S(1)}, bf16[2048,128]{1,0:T(8,128)(2,1)}, u32[]{:S(2)}, u32[]{:S(2)}) collective-permute-start(bf16[2048,128]{1,0:T(8,128)(2,1)S(1)} %get-tuple-element.59), channel_id=1, source_target_pairs={{0,1},{1,0},{2,3},{3,2},{4,5},{5,4},{6,7},{7,6},{8,9},{9,8},{10,11... | collective-permute-start | bytes 1572872 | tf_op jit(solution)/shard_map/ppermute | solution.py:638
  178.5 1.2 collective-permute-start.2
  178.7 73.5 %copy-start.51 = (f32[2048]{0:T(1024)}, f32[2048]{0:T(1024)S(1)}, u32[]{:S(2)}) copy-start(f32[2048]{0:T(1024)S(1)} %mul.134) | copy-start | bytes 24580
  179.8 78.9 %copy-start.49 = (f32[2048]{0:T(1024)}, f32[2048]{0:T(1024)S(1)}, u32[]{:S(2)}) copy-start(f32[2048]{0:T(1024)S(1)} %broadcast_in_dim_reshape.4) | copy-start | bytes 24580
  182.2 70.1 %copy-start.33 = (f32[2,256,256]{2,1,0:T(8,128)S(1)}, f32[2,256,256]{2,1,0:T(8,128)}, u32[]{:S(2)}) copy-start(f32[2,256,256]{2,1,0:T(8,128)} %copy-done.32) | copy-start | bytes 1572868
  182.2 79.2 %collective-permute-start.3 = (bf16[2048,128]{1,0:T(8,128)(2,1)}, bf16[2048,128]{1,0:T(8,128)(2,1)S(1)}, u32[]{:S(2)}, u32[]{:S(2)}) collective-permute-start(bf16[2048,128]{1,0:T(8,128)(2,1)} %fusion.13), channel_id=1, source_target_pairs={{0,2},{1,3},{4,6},{5,7},{8,10},{9,11},{12,14},{13,15},{16,18},{17,... | collective-permute-start | bytes 1572872 | tf_op jit(solution)/shard_map/ppermute | solution.py:647
  245.1 7.1 %copy-start.6 = (bf16[512,2048]{1,0:T(8,128)(2,1)S(1)}, bf16[512,2048]{1,0:T(8,128)(2,1)}, u32[]{:S(2)}) copy-start(bf16[512,2048]{1,0:T(8,128)(2,1)} %copy-done.5) | copy-start | bytes 6291460
  258.7 2.0 copy-start.4
  263.7 29.9 %copy-start.41 = (bf16[528,1024]{1,0:T(8,128)(2,1)S(1)}, bf16[528,1024]{1,0:T(8,128)(2,1)}, u32[]{:S(2)}) copy-start(bf16[528,1024]{1,0:T(8,128)(2,1)} %copy-done.40) | copy-start | bytes 3244036
  297.9 178.1 %reduce-scatter.8.cloned.1.call-start = ((), (), s32[]{:S(2)}) async-start(), calls=%async_computation.8 | async-start | bytes 4718592 | tf_op jit(solution)/shard_map/reduce_scatter | solution.py:671
  304.3 2.3 copy-start.50
  304.3 270.3 %reduce-scatter.6.cloned.1.call-start = ((), (), s32[]{:S(2)}) async-start(), calls=%async_computation.7 | async-start | bytes 5308416 | tf_op jit(solution)/shard_map/reduce_scatter | solution.py:671
  304.3 2.2 collective-permute-start.4
  308.2 19.7 %collective-permute-start.5 = (bf16[2048,128]{1,0:T(8,128)(2,1)S(1)}, bf16[2048,128]{1,0:T(8,128)(2,1)S(1)}, u32[]{:S(2)}, u32[]{:S(2)}) collective-permute-start(bf16[2048,128]{1,0:T(8,128)(2,1)S(1)} %fusion.15), channel_id=1, source_target_pairs={{2,0},{3,1},{6,4},{7,5},{10,8},{11,9},{14,12},{15,13},{18,16},{19,... | collective-permute-start | bytes 1572872 | tf_op jit(solution)/shard_map/ppermute | solution.py:647
  309.7 1.6 copy-start.7
  311.3 1.6 copy-start.10
  314.9 13.0 %copy-start.54 = (f32[2048]{0:T(1024)S(1)}, f32[2048]{0:T(1024)}, u32[]{:S(2)}) copy-start(f32[2048]{0:T(1024)} %get-tuple-element.127) | copy-start | bytes 24580
  314.9 13.4 %copy-start.8 = (bf16[512,2048]{1,0:T(8,128)(2,1)S(1)}, bf16[512,2048]{1,0:T(8,128)(2,1)}, u32[]{:S(2)}) copy-start(bf16[512,2048]{1,0:T(8,128)(2,1)} %copy-done.5) | copy-start | bytes 6291460
  314.9 13.4 %copy-start.14 = (f32[512,32]{1,0:T(8,128)S(1)}, f32[512,32]{1,0:T(8,128)}, u32[]{:S(2)}) copy-start(f32[512,32]{1,0:T(8,128)} %copy-done.13) | copy-start | bytes 196612
  314.9 13.4 %copy-start.16 = (f32[512,128]{1,0:T(8,128)S(1)}, f32[512,128]{1,0:T(8,128)}, u32[]{:S(2)}) copy-start(f32[512,128]{1,0:T(8,128)} %copy-done.15) | copy-start | bytes 786436
  314.9 13.4 %copy-start.19 = (bf16[512,128]{1,0:T(8,128)(2,1)S(1)}, bf16[512,128]{1,0:T(8,128)(2,1)}, u32[]{:S(2)}) copy-start(bf16[512,128]{1,0:T(8,128)(2,1)} %copy-done.17) | copy-start | bytes 393220
  314.9 13.4 %copy-start.21 = (bf16[512,96]{1,0:T(8,128)(2,1)S(1)}, bf16[512,96]{1,0:T(8,128)(2,1)}, u32[]{:S(2)}) copy-start(bf16[512,96]{1,0:T(8,128)(2,1)} %copy-done.20) | copy-start | bytes 294916
  325.8 2.1 copy-start.3
  327.9 1.6 copy-start.27
  329.5 31.6 %copy-start.42 = (bf16[528,1024]{1,0:T(8,128)(2,1)S(1)}, bf16[528,1024]{1,0:T(8,128)(2,1)}, u32[]{:S(2)}) copy-start(bf16[528,1024]{1,0:T(8,128)(2,1)} %copy-done.40) | copy-start | bytes 3244036
  357.2 3.9 copy-start.22
  357.2 3.3 collective-permute-start.6
  367.2 4.2 copy-start.31
  367.2 280.5 %all-reduce.5.cloned.1.call-start = ((), (), s32[]{:S(2)}) async-start(), calls=%async_computation.9 | async-start | bytes 196608
  368.7 8.6 %copy-start.55 = (f32[512]{0:T(512)}, f32[512]{0:T(512)S(1)}, u32[]{:S(2)}) copy-start(f32[512]{0:T(512)S(1)} %fusion.4) | copy-start | bytes 6148
  371.4 7.3 %copy-start.23 = (bf16[512,32]{1,0:T(8,128)(2,1)S(1)}, bf16[512,32]{1,0:T(8,128)(2,1)}, u32[]{:S(2)}) copy-start(bf16[512,32]{1,0:T(8,128)(2,1)} %copy-done.22) | copy-start | bytes 98308
  382.3 5.4 copy-start.38
  382.3 5.4 copy-start.45
  382.3 5.4 copy-start.53
  387.8 4.5 copy-start.29
  392.2 182.4 %copy-start.56 = (f32[512]{0:T(512)S(1)}, f32[512]{0:T(512)}, u32[]{:S(2)}) copy-start(f32[512]{0:T(512)} %copy-done.55) | copy-start | bytes 6148
  392.2 182.4 %copy-start.57 = (f32[512]{0:T(512)S(1)}, f32[512]{0:T(512)}, u32[]{:S(2)}) copy-start(f32[512]{0:T(512)} %get-tuple-element.117) | copy-start | bytes 6148
  392.2 301.5 %all-reduce.7.cloned.1.call-start = ((), (), s32[]{:S(2)}) async-start(), calls=%async_computation.10 | async-start | bytes 3276800 | tf_op jit(solution)/shard_map/psum | solution.py:672
  397.8 176.8 %copy-start.43 = (bf16[1,512,1024]{2,1,0:T(8,128)(2,1)S(1)}, bf16[1,512,1024]{2,1,0:T(8,128)(2,1)}, u32[]{:S(2)}) copy-start(bf16[1,512,1024]{2,1,0:T(8,128)(2,1)} %param.14) | copy-start | bytes 3145732
  695.2 2.0 copy-start.46
  (18 other events, 20.1 us)
Sparse Core Ops, SparseCore 0:
  10.7 84.7 all-gather.4
  98.1 73.1 all-gather.6
  173.5 71.5 all-gather.8
  298.1 86.1 reduce-scatter.3
  388.2 87.8 reduce-scatter.7
  479.5 95.0 reduce-scatter.5
  578.5 69.1 all-reduce.4
  650.3 43.3 all-reduce.6
